TPU v7x, 32 devices: a whole 2x2x4 slice. The times are simulated.
32 devices in a mesh: dp: 4 (over x, core), ctx: 8 (over z, y).
Axes of the slice: x: 2, y: 2, z: 4, core: 2. Of those that a mesh axis runs over, the one named last changes fastest.
Arguments:
- queries: bfloat16 [4, 1024, 2048], P('dp', 'ctx'), may hold values from -6 to 6
- keys: bfloat16 [4, 1024, 2048], P('dp', 'ctx'), may hold values from -6 to 6
- values: bfloat16 [4, 1024, 2048], P('dp', 'ctx'), may hold values from -6 to 6
- cotangent: bfloat16 [4, 1024, 2048], P('dp', 'ctx'), may hold values from -6 to 6
- doc_lengths: int32 [4, 4], P('dp'), may hold values from 0 to 1024, as said below
- filter_taps: float32 [1024, 2048], P('ctx'), may hold values from -0.1875 to 0.1875
Outputs:
- hyena_out: bfloat16 [4, 1024, 2048], P('dp', 'ctx')
- grad_queries: bfloat16 [4, 1024, 2048], P('dp', 'ctx')
- grad_keys: bfloat16 [4, 1024, 2048], P('dp', 'ctx')
- grad_values: bfloat16 [4, 1024, 2048], P('dp', 'ctx')
- grad_filter: float32 [1024, 2048], P('ctx', 'dp')
Inputs may be any that keep to these rules, and one draw needn't show every extreme that they name: `doc_lengths`: each row holds 4 document lengths that sum to 1024; a length may be zero (an unused slot); in every draw some row holds a single document of all 1024 positions.
All inputs are finite; a program needn't handle non-finite values.
Results may differ from a plain program's by a relative error of at most 0.0051.
Values may be sent and summed in bfloat16 or wider, within the bound.
A program may use at most 512 MiB of HBM per device.

v0:
```python
import math

import jax
import jax.numpy as jnp
from jax import lax
from jax.sharding import PartitionSpec as P


def matmul(matrix, operand):
    return jnp.dot(
        matrix, operand, precision=lax.Precision.HIGHEST, preferred_element_type=jnp.float32
    )


def tables(block_len):
    period = 2 * block_len
    freqs = block_len + 1
    freq_row = lax.broadcasted_iota(jnp.int32, (freqs, period), 0)
    pos_col = lax.broadcasted_iota(jnp.int32, (freqs, period), 1)
    phase_angle = (freq_row * pos_col % period).astype(jnp.float32) * (2.0 * math.pi / period)
    pos_row = lax.broadcasted_iota(jnp.int32, (period, freqs), 0)
    freq_col = lax.broadcasted_iota(jnp.int32, (period, freqs), 1)
    rolled_index = (pos_row + block_len) % period * freq_col % period
    rolled_angle = rolled_index.astype(jnp.float32) * (2.0 * math.pi / period)
    weight_col = (
        jnp.where((freq_col == 0) | (freq_col == block_len), 1.0, 2.0).astype(jnp.float32) / period
    )
    return (
        jnp.cos(phase_angle),
        -jnp.sin(phase_angle),
        weight_col * jnp.cos(rolled_angle),
        weight_col * jnp.sin(rolled_angle),
    )


def doc_ids(positions, doc_ends):
    return jnp.sum((doc_ends[None, :] <= positions[:, None]).astype(jnp.int32), axis=1)


def spectrum(rows_in, keep_rows, dft_tables):
    half_len = rows_in.shape[0]
    masked = rows_in.astype(jnp.float32) * keep_rows.astype(jnp.float32)[:, None]
    return (
        matmul(dft_tables[0][:, :half_len], masked),
        matmul(dft_tables[1][:, :half_len], masked),
    )


def window_spectrum(padded_filter, lag_block, dft_tables, block_len):
    window = lax.dynamic_slice_in_dim(padded_filter, lag_block * block_len, 2 * block_len, 0)
    return (matmul(dft_tables[0], window), matmul(dft_tables[1], window))


def inverse_upper(spec_real, spec_imag, dft_tables):
    half_len = dft_tables[2].shape[0] // 2
    return matmul(dft_tables[2][:half_len], spec_real) - matmul(dft_tables[3][:half_len], spec_imag)


def inverse_full(spec_real, spec_imag, dft_tables):
    return matmul(dft_tables[2], spec_real) - matmul(dft_tables[3], spec_imag)


def add_lags(buffer, segment, lag_block, half_len):
    start_row = lag_block * half_len
    current = lax.dynamic_slice_in_dim(buffer, start_row, 2 * half_len, 0)
    return lax.dynamic_update_slice_in_dim(buffer, current + segment, start_row, 0)


def body(queries, keys, values, cotangent, doc_lengths, filter_taps):
    block_len = queries.shape[1]
    channels = queries.shape[2]
    doc_count = doc_lengths.shape[1]
    ctx_size = lax.axis_size("ctx")
    ctx_rank = lax.axis_index("ctx")
    dft_tables = tables(block_len)
    lengths = doc_lengths[0]
    doc_ends = jnp.cumsum(lengths)
    doc_starts = doc_ends - lengths
    local_pos = lax.broadcasted_iota(jnp.int32, (block_len,), 0)
    own_docs = doc_ids(ctx_rank * block_len + local_pos, doc_ends)
    first_doc = own_docs[0]
    last_doc = own_docs[block_len - 1]
    first_start = doc_starts[first_doc]
    last_end = doc_ends[last_doc]
    query_f = queries[0].astype(jnp.float32)
    key_f = keys[0].astype(jnp.float32)
    value_f = values[0].astype(jnp.float32)
    cot_f = cotangent[0].astype(jnp.float32)
    gated_input = (key_f * value_f).astype(jnp.bfloat16)
    weighted = (cot_f * query_f).astype(jnp.bfloat16)
    filter_all = lax.all_gather(filter_taps, "ctx", axis=0, tiled=True)
    padded_filter = jnp.concatenate(
        [jnp.zeros((block_len, channels), jnp.float32), filter_all], axis=0
    )
    head_keep = own_docs == first_doc
    tail_keep = own_docs == last_doc
    head_real, head_imag = spectrum(weighted, head_keep, dft_tables)
    diag_real, diag_imag = window_spectrum(padded_filter, 0, dft_tables, block_len)
    freqs = block_len + 1
    zero_rows = jnp.zeros((block_len, channels), jnp.float32)
    zero_spec = jnp.zeros((freqs, channels), jnp.float32)
    zero_segment = jnp.zeros((2 * block_len, channels), jnp.float32)
    diag_state = (zero_rows, zero_rows, zero_spec, zero_spec)
    for doc_index in range(doc_count):
        touches = (doc_starts[doc_index] < (ctx_rank + 1) * block_len) & (
            doc_ends[doc_index] > ctx_rank * block_len
        )

        def doc_work(current, doc_index=doc_index):
            conv_rows, adj_rows, cross_real, cross_imag = current
            keep_rows = own_docs == doc_index
            keep_col = keep_rows.astype(jnp.float32)[:, None]
            in_real, in_imag = spectrum(gated_input, keep_rows, dft_tables)
            wt_real, wt_imag = spectrum(weighted, keep_rows, dft_tables)
            conv_rows = conv_rows + keep_col * inverse_upper(
                diag_real * in_real - diag_imag * in_imag,
                diag_real * in_imag + diag_imag * in_real,
                dft_tables,
            )
            adj_rows = adj_rows + keep_col * inverse_upper(
                diag_real * wt_real + diag_imag * wt_imag,
                diag_real * wt_imag - diag_imag * wt_real,
                dft_tables,
            )
            cross_real = cross_real + wt_real * in_real + wt_imag * in_imag
            cross_imag = cross_imag + wt_imag * in_real - wt_real * in_imag
            return (conv_rows, adj_rows, cross_real, cross_imag)

        diag_state = lax.cond(touches, doc_work, lambda current: current, diag_state)
    conv_rows, adj_rows, cross_real, cross_imag = diag_state
    lag_buffer = jnp.zeros(((ctx_size + 1) * block_len, channels), jnp.float32)
    lag_buffer = add_lags(
        lag_buffer, inverse_full(cross_real, cross_imag, dft_tables), 0, block_len
    )
    shard_rows = lax.all_gather(gated_input, "ctx", axis=0, tiled=True)
    first_row = jnp.int32(0)
    acc_real = zero_spec
    acc_imag = zero_spec
    lag_rows = lag_buffer
    shard_count = shard_rows.shape[0] // block_len
    for offset in range(shard_count):
        source = first_row // block_len + offset
        distance = ctx_rank - source
        safe_distance = jnp.clip(distance, 0, ctx_size - 1)
        sub_block = shard_rows[offset * block_len : (offset + 1) * block_len]
        linked = (distance >= 1) & (first_start < (source + 1) * block_len)

        def forward_pair_work(
            current, source=source, safe_distance=safe_distance, sub_block=sub_block
        ):
            run_real, run_imag = current
            keep_rows = doc_ids(source * block_len + local_pos, doc_ends) == first_doc
            src_real, src_imag = spectrum(sub_block, keep_rows, dft_tables)
            filt_real, filt_imag = window_spectrum(
                padded_filter, safe_distance, dft_tables, block_len
            )
            run_real = run_real + filt_real * src_real - filt_imag * src_imag
            run_imag = run_imag + filt_real * src_imag + filt_imag * src_real
            seg_real = head_real * src_real + head_imag * src_imag
            seg_imag = head_imag * src_real - head_real * src_imag
            segment = inverse_full(seg_real, seg_imag, dft_tables)
            return (run_real, run_imag, segment)

        def forward_skip_work(current):
            return (current[0], current[1], zero_segment)

        acc_real, acc_imag, segment = lax.cond(
            linked, forward_pair_work, forward_skip_work, (acc_real, acc_imag)
        )
        lag_rows = add_lags(lag_rows, segment, safe_distance, block_len)
    fwd_real = acc_real
    fwd_imag = acc_imag
    shard_rows = lax.all_gather(weighted, "ctx", axis=0, tiled=True)
    first_row = jnp.int32(0)
    acc_real = zero_spec
    acc_imag = zero_spec
    shard_count = shard_rows.shape[0] // block_len
    for offset in range(shard_count):
        target = first_row // block_len + offset
        distance = target - ctx_rank
        safe_distance = jnp.clip(distance, 0, ctx_size - 1)
        sub_block = shard_rows[offset * block_len : (offset + 1) * block_len]
        linked = (distance >= 1) & (last_end > target * block_len)

        def adjoint_pair_work(
            current, target=target, safe_distance=safe_distance, sub_block=sub_block
        ):
            run_real, run_imag = current
            keep_rows = doc_ids(target * block_len + local_pos, doc_ends) == last_doc
            tgt_real, tgt_imag = spectrum(sub_block, keep_rows, dft_tables)
            filt_real, filt_imag = window_spectrum(
                padded_filter, safe_distance, dft_tables, block_len
            )
            run_real = run_real + filt_real * tgt_real + filt_imag * tgt_imag
            run_imag = run_imag + filt_real * tgt_imag - filt_imag * tgt_real
            return (run_real, run_imag, zero_segment)

        def adjoint_skip_work(current):
            return (current[0], current[1], zero_segment)

        acc_real, acc_imag, segment = lax.cond(
            linked, adjoint_pair_work, adjoint_skip_work, (acc_real, acc_imag)
        )
    conv_rows = conv_rows + head_keep.astype(jnp.float32)[:, None] * inverse_upper(
        fwd_real, fwd_imag, dft_tables
    )
    adj_rows = adj_rows + tail_keep.astype(jnp.float32)[:, None] * inverse_upper(
        acc_real, acc_imag, dft_tables
    )
    hyena_out = (query_f * conv_rows).astype(jnp.bfloat16)
    grad_queries = (cot_f * conv_rows).astype(jnp.bfloat16)
    grad_keys = (adj_rows * value_f).astype(jnp.bfloat16)
    grad_values = (adj_rows * key_f).astype(jnp.bfloat16)
    grad_local = lag_rows[block_len:]
    lag_share = lax.psum_scatter(grad_local, "ctx", scatter_dimension=0, tiled=True)
    grad_filter = lax.psum_scatter(lag_share, "dp", scatter_dimension=1, tiled=True)
    return (hyena_out[None], grad_queries[None], grad_keys[None], grad_values[None], grad_filter)


def solution(mesh):
    in_specs = (
        P("dp", "ctx", None),
        P("dp", "ctx", None),
        P("dp", "ctx", None),
        P("dp", "ctx", None),
        P("dp", None),
        P("ctx", None),
    )
    out_specs = (
        P("dp", "ctx", None),
        P("dp", "ctx", None),
        P("dp", "ctx", None),
        P("dp", "ctx", None),
        P("ctx", "dp"),
    )
    return jax.shard_map(body, mesh=mesh, in_specs=in_specs, out_specs=out_specs, check_vma=False)
```

profile of v0, /device:TPU:3, one launch (start us, length us, event | category | flops | bytes accessed | tf_op | source)
XLA Modules:
  0.0 783.1 jit_solution(16225474035318065384)
XLA Ops:
  26.5 1.7 compare_convert_fusion.20
  28.2 2.0 sine_multiply_fusion
  32.7 103.2 %all-gather.4.cloned.1.call-done = f32[1024,2048]{1,0:T(8,128)} async-done(((f32[128,2048]{1,0:T(8,128)}), f32[1024,2048]{1,0:T(8,128)}) %all-gather.4.cloned.1.call-update) | async-done | bytes 8388624 | tf_op jit(solution)/shard_map/all_gather | solution.py:91
  135.9 3.0 fusion.374
  139.7 1.6 fusion.376
  142.3 23.9 %conditional.20 = (f32[128,2048]{0,1:T(8,128)}, f32[128,2048]{0,1:T(8,128)}, f32[129,2048]{1,0:T(8,128)}, f32[129,2048]{1,0:T(8,128)}) conditional(s32[]{:T(128)} %convert_element_type.626, () %tuple.148, (s32[128]{0:T(128)S(1)}, bf16[128,2048]{1,0:T(8,128)(2,1)S(1)}, f32[129,256]{1,0:T(8,128)S(1)}, f32[129,256]{1,0:T(8,128)S(1)}, ...), branch_computations={%region_2.3_spmd, %region_3.4_spmd} | conditional | flops 3254292736 | bytes 36704288 | solution.py:129
  146.3 2.9 multiply_subtract_fusion
  149.2 3.6 fusion.7
  152.8 5.0 fusion.1
  157.8 3.6 fusion.14
  161.4 4.6 fusion.3
  166.2 14.1 %conditional.21 = ((f32[128,2048]{0,1:T(8,128)}, f32[128,2048]{0,1:T(8,128)}, f32[129,2048]{1,0:T(8,128)}, f32[129,2048]{1,0:T(8,128)})) conditional(s32[]{:T(128)} %convert_element_type.625, (f32[128,2048]{0,1:T(8,128)}, f32[128,2048]{0,1:T(8,128)}, f32[129,2048]{1,0:T(8,128)}, f32[129,2048]{1,0:T(8,128)}) %conditional.20, (s32[128]{0:T(128)S(1)}, ...), branch_computations={%region_4.5_spmd, %region_5.6_spmd} | conditional | flops 3255345408 | bytes 50921680 | solution.py:129
  180.3 14.3 %conditional.22 = ((f32[128,2048]{0,1:T(8,128)}, f32[128,2048]{0,1:T(8,128)}, f32[129,2048]{1,0:T(8,128)}, f32[129,2048]{1,0:T(8,128)})) conditional(s32[]{:T(128)} %convert_element_type.624, (f32[128,2048]{0,1:T(8,128)}, f32[128,2048]{0,1:T(8,128)}, f32[129,2048]{1,0:T(8,128)}, f32[129,2048]{1,0:T(8,128)}) %get-tuple-element.1245, ...), branch_computations={%region_6.7_spmd, %region_7.8_spmd} | conditional | flops 3255345408 | bytes 50921680 | solution.py:129
  194.6 11.4 %conditional.23 = (f32[129,2048]{1,0:T(8,128)}, f32[129,2048]{1,0:T(8,128)}, f32[128,2048]{1,0:T(8,128)S(1)}, f32[128,2048]{1,0:T(8,128)}) conditional(s32[]{:T(128)} %convert_element_type.623, (f32[128,2048]{0,1:T(8,128)}, f32[128,2048]{0,1:T(8,128)}, f32[129,2048]{1,0:T(8,128)}, f32[129,2048]{1,0:T(8,128)}) %get-tuple-element.1246, ...), branch_computations={%region_8.9_spmd, %region_9.10_spmd} | conditional | flops 3255345408 | bytes 76722544 | solution.py:129
  196.2 2.6 copy.33
  205.9 4.5 fusion.411
  210.4 4.2 convolution_subtract_fusion.16
  216.1 4.7 dynamic_update_slice.27
  220.8 4.4 concatenate.3
  225.2 12.3 %conditional.24 = (f32[129,2048]{1,0:T(8,128)S(1)}, f32[129,2048]{1,0:T(8,128)}, f32[256,2048]{1,0:T(8,128)}) conditional(s32[]{:T(128)} %convert_element_type.646, () %tuple.153, (s32[]{:T(128)}, f32[1152,2048]{1,0:T(8,128)}, f32[129,256]{1,0:T(8,128)S(1)}, bf16[1024,2048]{1,0:T(8,128)(2,1)}, s32[4]{0:T(128)S(1)}, /*index=5*/s32[128]{0:T(128)S(1)}, ...), branch_computations={%region_10.11_spmd, %region_11.13_spmd} | conditional | flops 4062733824 | bytes 34892984 | solution.py:167
  237.5 10.9 %conditional.25 = (f32[129,2048]{1,0:T(8,128)S(1)}, f32[129,2048]{1,0:T(8,128)}, f32[256,2048]{1,0:T(8,128)}) conditional(s32[]{:T(128)} %convert_element_type.645, (f32[129,2048]{1,0:T(8,128)S(1)}, f32[129,2048]{1,0:T(8,128)}) %tuple.155, (s32[]{:T(128)}, f32[1152,2048]{1,0:T(8,128)}, f32[129,256]{1,0:T(8,128)S(1)}, ...), branch_computations={%region_13.14_spmd, %region_14.16_spmd} | conditional | flops 4063262464 | bytes 37064888 | solution.py:167
  248.4 9.6 %conditional.26 = (f32[129,2048]{1,0:T(8,128)S(1)}, f32[129,2048]{1,0:T(8,128)}, f32[256,2048]{1,0:T(8,128)}) conditional(s32[]{:T(128)} %convert_element_type.644, (f32[129,2048]{1,0:T(8,128)S(1)}, f32[129,2048]{1,0:T(8,128)}) %tuple.157, (s32[]{:T(128)}, f32[1152,2048]{1,0:T(8,128)}, f32[129,256]{1,0:T(8,128)S(1)}, ...), branch_computations={%region_16.17_spmd, %region_17.19_spmd} | conditional | flops 4063262464 | bytes 37064888 | solution.py:167
  258.0 9.3 %conditional.27 = (f32[129,2048]{1,0:T(8,128)S(1)}, f32[129,2048]{1,0:T(8,128)}, f32[256,2048]{1,0:T(8,128)}) conditional(s32[]{:T(128)} %convert_element_type.643, (f32[129,2048]{1,0:T(8,128)S(1)}, f32[129,2048]{1,0:T(8,128)}) %tuple.159, (s32[]{:T(128)}, f32[1152,2048]{1,0:T(8,128)}, f32[129,256]{1,0:T(8,128)S(1)}, ...), branch_computations={%region_19.20_spmd, %region_20.22_spmd} | conditional | flops 4063262464 | bytes 37064888 | solution.py:167
  267.4 9.6 %conditional.28 = (f32[129,2048]{1,0:T(8,128)S(1)}, f32[129,2048]{1,0:T(8,128)}, f32[256,2048]{1,0:T(8,128)}) conditional(s32[]{:T(128)} %convert_element_type.642, (f32[129,2048]{1,0:T(8,128)S(1)}, f32[129,2048]{1,0:T(8,128)}) %tuple.161, (s32[]{:T(128)}, f32[1152,2048]{1,0:T(8,128)}, f32[129,256]{1,0:T(8,128)S(1)}, ...), branch_computations={%region_22.23_spmd, %region_23.25_spmd} | conditional | flops 4063262464 | bytes 37064888 | solution.py:167
  276.9 9.3 %conditional.29 = (f32[129,2048]{1,0:T(8,128)S(1)}, f32[129,2048]{1,0:T(8,128)}, f32[256,2048]{1,0:T(8,128)}) conditional(s32[]{:T(128)} %convert_element_type.641, (f32[129,2048]{1,0:T(8,128)S(1)}, f32[129,2048]{1,0:T(8,128)}) %tuple.163, (s32[]{:T(128)}, f32[1152,2048]{1,0:T(8,128)}, f32[129,256]{1,0:T(8,128)S(1)}, ...), branch_computations={%region_25.26_spmd, %region_26.28_spmd} | conditional | flops 4063262464 | bytes 37064888 | solution.py:167
  286.3 6.9 conditional.30
  293.2 4.0 fusion.373
  297.2 4.0 add_dynamic-update-slice_fusion.6
  301.2 4.0 add_dynamic-update-slice_fusion.5
  305.1 4.0 add_dynamic-update-slice_fusion.4
  309.1 4.0 add_dynamic-update-slice_fusion.3
  313.1 4.0 add_dynamic-update-slice_fusion.2
  317.1 4.0 add_dynamic-update-slice_fusion.1
  321.3 3.6 add_dynamic-update-slice_fusion
  324.8 7.8 slice.337
  333.2 272.6 %reduce-scatter.3.cloned.1.call-done = f32[128,2048]{1,0:T(8,128)} async-done(((f32[1024,2048]{1,0:T(8,128)}), f32[128,2048]{1,0:T(8,128)}) %reduce-scatter.3.cloned.1.call-update) | async-done | bytes 1048592 | tf_op jit(solution)/shard_map/reduce_scatter | solution.py:215
  611.0 68.8 %all-gather.8.cloned.1.call-done = bf16[1024,2048]{1,0:T(8,128)(2,1)} async-done(((bf16[128,2048]{1,0:T(8,128)(2,1)}), bf16[1024,2048]{1,0:T(8,128)(2,1)}) %all-gather.8.cloned.1.call-update) | async-done | bytes 4194320 | tf_op jit(solution)/shard_map/all_gather | solution.py:173
  679.8 3.7 fusion.432
  684.8 11.1 %conditional.33 = ((f32[129,2048]{1,0:T(8,128)S(1)}, f32[129,2048]{1,0:T(8,128)})) conditional(s32[]{:T(128)} %convert_element_type.657, (f32[129,2048]{1,0:T(8,128)S(1)}, f32[129,2048]{1,0:T(8,128)}) %conditional.32, (s32[]{:T(128)}, f32[1152,2048]{1,0:T(8,128)}, f32[129,256]{1,0:T(8,128)S(1)}, bf16[128,2048]{1,0:T(8,128)(2,1)}, s32[4]{0:T(128)S(1)}, ...), branch_computations={%region_37.38_spmd, %region_38.40_spmd} | conditional | flops 2437957376 | bytes 18901146 | solution.py:201
  684.8 3.0 fusion.284
  691.0 4.9 bitcast_subtract_fusion
  695.9 11.5 %conditional.34 = ((f32[129,2048]{1,0:T(8,128)S(1)}, f32[129,2048]{1,0:T(8,128)})) conditional(s32[]{:T(128)} %convert_element_type.656, (f32[129,2048]{1,0:T(8,128)S(1)}, f32[129,2048]{1,0:T(8,128)}) %get-tuple-element.1247, (s32[]{:T(128)}, f32[1152,2048]{1,0:T(8,128)}, f32[129,256]{1,0:T(8,128)S(1)}, bf16[128,2048]{1,0:T(8,128)(2,1)}, ...), branch_computations={%region_40.41_spmd, %region_41.43_spmd} | conditional | flops 2437957376 | bytes 18901146 | solution.py:201
  696.3 3.0 fusion.296
  702.6 4.8 bitcast_subtract_fusion.1
  707.4 11.1 %conditional.35 = ((f32[129,2048]{1,0:T(8,128)S(1)}, f32[129,2048]{1,0:T(8,128)})) conditional(s32[]{:T(128)} %convert_element_type.655, (f32[129,2048]{1,0:T(8,128)S(1)}, f32[129,2048]{1,0:T(8,128)}) %get-tuple-element.1248, (s32[]{:T(128)}, f32[1152,2048]{1,0:T(8,128)}, f32[129,256]{1,0:T(8,128)S(1)}, bf16[128,2048]{1,0:T(8,128)(2,1)}, ...), branch_computations={%region_43.44_spmd, %region_44.46_spmd} | conditional | flops 2437957376 | bytes 18901146 | solution.py:201
  707.4 3.0 fusion.308
  713.7 4.8 bitcast_subtract_fusion.2
  718.5 11.2 %conditional.36 = ((f32[129,2048]{1,0:T(8,128)S(1)}, f32[129,2048]{1,0:T(8,128)})) conditional(s32[]{:T(128)} %convert_element_type.654, (f32[129,2048]{1,0:T(8,128)S(1)}, f32[129,2048]{1,0:T(8,128)}) %get-tuple-element.1249, (s32[]{:T(128)}, f32[1152,2048]{1,0:T(8,128)}, f32[129,256]{1,0:T(8,128)S(1)}, bf16[128,2048]{1,0:T(8,128)(2,1)}, ...), branch_computations={%region_46.47_spmd, %region_47.49_spmd} | conditional | flops 2437957376 | bytes 18901146 | solution.py:201
  718.7 3.0 fusion.320
  725.0 4.8 bitcast_subtract_fusion.3
  729.8 11.1 %conditional.37 = ((f32[129,2048]{1,0:T(8,128)S(1)}, f32[129,2048]{1,0:T(8,128)})) conditional(s32[]{:T(128)} %convert_element_type.653, (f32[129,2048]{1,0:T(8,128)S(1)}, f32[129,2048]{1,0:T(8,128)}) %get-tuple-element.1250, (s32[]{:T(128)}, f32[1152,2048]{1,0:T(8,128)}, f32[129,256]{1,0:T(8,128)S(1)}, bf16[128,2048]{1,0:T(8,128)(2,1)}, ...), branch_computations={%region_49.50_spmd, %region_50.52_spmd} | conditional | flops 2437957376 | bytes 18901146 | solution.py:201
  729.8 3.0 fusion.332
  736.0 4.8 bitcast_subtract_fusion.4
  740.9 11.2 %conditional.38 = ((f32[129,2048]{1,0:T(8,128)S(1)}, f32[129,2048]{1,0:T(8,128)})) conditional(s32[]{:T(128)} %convert_element_type.652, (f32[129,2048]{1,0:T(8,128)S(1)}, f32[129,2048]{1,0:T(8,128)}) %get-tuple-element.1251, (s32[]{:T(128)}, f32[1152,2048]{1,0:T(8,128)}, f32[129,256]{1,0:T(8,128)S(1)}, bf16[128,2048]{1,0:T(8,128)(2,1)S(1)}, ...), branch_computations={%region_52.53_spmd, %region_53.55_spmd} | conditional | flops 2437957376 | bytes 16803966 | solution.py:201
  741.1 2.9 fusion.344
  747.3 4.8 bitcast_subtract_fusion.5
  752.1 13.3 %conditional.39 = ((f32[129,2048]{1,0:T(8,128)S(1)}, f32[129,2048]{1,0:T(8,128)})) conditional(s32[]{:T(128)} %convert_element_type.651, (f32[129,2048]{1,0:T(8,128)S(1)}, f32[129,2048]{1,0:T(8,128)}) %get-tuple-element.1252, (s32[]{:T(128)}, f32[1152,2048]{1,0:T(8,128)}, f32[129,256]{1,0:T(8,128)S(1)}, bf16[1024,2048]{1,0:T(8,128)(2,1)}, ...), branch_computations={%region_55.56_spmd, %region_56.58_spmd} | conditional | flops 2437957376 | bytes 16803990 | solution.py:201
  752.1 2.9 fusion.356
  755.8 2.3 fusion.358
  758.1 2.3 fusion.359
  760.4 4.8 bitcast_subtract_fusion.6
  765.5 2.0 fusion.403
  768.9 3.6 fusion.388
  772.6 3.5 fusion.386
  (179 shorter events, 53.1 us)
Async XLA Ops:
  7.2 1.0 copy-start.81
  7.2 1.2 copy-start.83
  7.2 128.8 %all-gather.4.cloned.1.call-start = ((), (), s32[]{:S(2)}) async-start(), calls=%async_computation.2 | async-start | bytes 9437184 | tf_op jit(solution)/shard_map/all_gather | solution.py:91
  7.9 1.5 copy-start.88
  7.9 217.3 %all-gather.6.cloned.1.call-start = ((), (), s32[]{:S(2)}) async-start(), calls=%async_computation.3 | async-start | bytes 4718592 | tf_op jit(solution)/shard_map/all_gather | solution.py:135
  9.3 21.0 %copy-start.77 = (bf16[1,128,2048]{2,1,0:T(8,128)(2,1)S(1)}, bf16[1,128,2048]{2,1,0:T(8,128)(2,1)}, u32[]{:S(2)}) copy-start(bf16[1,128,2048]{2,1,0:T(8,128)(2,1)} %param.49) | copy-start | bytes 1572868
  9.3 21.0 %copy-start.79 = (bf16[1,128,2048]{2,1,0:T(8,128)(2,1)S(1)}, bf16[1,128,2048]{2,1,0:T(8,128)(2,1)}, u32[]{:S(2)}) copy-start(bf16[1,128,2048]{2,1,0:T(8,128)(2,1)} %param.46) | copy-start | bytes 1572868
  9.3 596.6 %reduce-scatter.3.cloned.1.call-start = ((), (), s32[]{:S(2)}) async-start(), calls=%async_computation.5 | async-start | bytes 9437184 | tf_op jit(solution)/shard_map/reduce_scatter | solution.py:215
  26.5 5.1 copy-start.5
  28.2 3.3 copy-start.85
  30.4 2.3 copy-start.26
  135.9 3.7 copy-start.31
  139.6 1.7 copy-start.6
  139.6 1.7 copy-start.27
  139.6 1.7 copy-start.32
  139.6 1.7 copy-start.36
  139.7 1.7 copy-start.50
  141.3 1.0 copy-start
  205.9 4.5 copy-start.74
  210.4 10.3 %slice-start = ((s8[8388608]{0:T(1024)(128)(4,1)}), s8[4194304]{0:T(1024)(128)(4,1)S(1)}, s32[]{:S(2)}) async-start(s8[8388608]{0:T(1024)(128)(4,1)} %bitcast.337), calls=%async_computation.7 | async-start | bytes 8388608
  214.7 1.4 copy-start.63
  216.1 4.7 slice-start.1
  332.6 347.2 %all-gather.8.cloned.1.call-start = ((), (), s32[]{:S(2)}) async-start(), calls=%async_computation.4 | async-start | bytes 4718592 | tf_op jit(solution)/shard_map/all_gather | solution.py:173
  333.2 442.9 %reduce-scatter.5.cloned.1.call-start = ((), (), s32[]{:S(2)}) async-start(), calls=%async_computation.6 | async-start | bytes 1310720 | tf_op jit(solution)/shard_map/reduce_scatter | solution.py:216
  684.8 3.7 copy-start.19
  684.8 3.7 copy-start.72
  696.3 3.7 copy-start.20
  696.3 3.7 copy-start.71
  707.4 3.7 copy-start.21
  707.4 3.7 copy-start.70
  718.7 3.7 copy-start.22
  718.7 3.7 copy-start.69
  729.8 3.7 copy-start.23
  729.8 3.7 copy-start.68
  741.0 3.7 copy-start.24
  752.1 3.7 copy-start.25
  765.4 2.0 copy-start.51
  765.4 3.1 copy-start.80
  767.5 1.1 copy-start.37
  767.5 1.3 copy-start.75
  767.5 1.4 copy-start.78
  767.5 1.4 copy-start.86
  768.9 3.7 copy-start.76
  768.9 3.7 copy-start.82
  768.9 3.7 copy-start.84
  768.9 3.7 copy-start.87
Sparse Core Ops, SparseCore 0:
  10.1 125.7 all-gather.3
  138.6 70.7 all-gather.5
  332.7 273.0 reduce-scatter.2
  608.6 71.1 all-gather.7
  682.9 23.3 reduce-scatter.4
where the time goes:
time: 782 us; the launch traced here: 783 us
  waiting for transfers between devices  446 us (57%)
  matrix products  123 us (16%)
  loops' own time  93 us (12%)
  local copies, waits for them, and re-layouts  44.4 us (6%)
  other arithmetic  42 us (5%)
  between operations  34.1 us (4%)
    reduce_scatter x1, waiting for transfers between devices, body(): lax.psum_scatter(grad_local, 'ctx', scatter_dimension=0, tiled=True)  273 us
    dot_general x46, matrix products, matmul(): jnp.dot(matrix, operand, precision=lax.Precision.HIGHEST, preferred_eleme...  123 us
    all_gather x1, waiting for transfers between devices, body(): filter_all = lax.all_gather(filter_taps, 'ctx', axis=0, tiled=True)  103 us
    all_gather x1, waiting for transfers between devices, body(): shard_rows = lax.all_gather(weighted, 'ctx', axis=0, tiled=True)  68.8 us
    another operation x8, loops' own time, body(): lax.cond(linked, forward_pair_work, forward_skip_work, (acc_real, acc_imag))  55.7 us
    another operation x4, loops' own time, body(): lax.cond(touches, doc_work, lambda current: current, diag_state)  36 us
    dynamic_update_slice x8, other arithmetic, add_lags(): lax.dynamic_update_slice_in_dim(buffer, current + segment, start_row, 0)  31.4 us
  transfers between devices with their start and end apart: 5, of which 3 were waited for; matrix products, arithmetic and copies ran while one was open for 20% of the time, Pallas kernels for 0%

commit v1 on v0

v1 whole, which is shorter than its diff:
```python
import functools
import math

import jax
import jax.numpy as jnp
import numpy as np
import ml_dtypes
from jax import lax
from jax.experimental import pallas as pl
from jax.experimental.pallas import tpu as pltpu
from jax.sharding import PartitionSpec as P


def tables(block_len):
    turns = (2 * np.arange(block_len)[:, None] + 1) * np.arange(block_len)[None, :]
    angle = (turns % (4 * block_len)) * (2.0 * math.pi / (4 * block_len))
    forward = np.concatenate([np.cos(angle), -np.sin(angle)], axis=0)
    inverse = forward.T / block_len

    def split(table):
        high = table.astype(ml_dtypes.bfloat16)
        low = (table - high.astype(np.float64)).astype(ml_dtypes.bfloat16)
        return high, low

    fwd_high, fwd_low = split(forward)
    inv_high, inv_low = split(inverse)
    return (
        np.concatenate([fwd_high, fwd_low], axis=1),
        np.concatenate([inv_high, inv_high, inv_low], axis=1),
    )


def conv_kernel(
    lengths_ref, rows_ref, fwd_ref, inv_ref, conv_ref, lag_ref,
    in_spec, wt_spec, filt_spec, conv_spec, adj_spec, lag_spec, conv_acc, adj_acc,
):
    blocks, double, channels = in_spec.shape
    block_len = double // 2
    docs = lengths_ref.shape[1]
    row_id = lax.broadcasted_iota(jnp.int32, (block_len, channels), 0)
    sign = (1 - 2 * (row_id % 2)).astype(jnp.float32)
    chunk = 16

    def rows_at(block):
        return pl.ds(pl.multiple_of(block * block_len, block_len), block_len)

    def forward(rows):
        return jnp.dot(
            fwd_ref[...], jnp.concatenate([rows, rows], axis=0), preferred_element_type=jnp.float32
        )

    def inverse(spec):
        high = spec.astype(jnp.bfloat16)
        low = (spec - high.astype(jnp.float32)).astype(jnp.bfloat16)
        return jnp.dot(
            inv_ref[...], jnp.concatenate([high, low, high], axis=0),
            preferred_element_type=jnp.float32,
        )

    @pl.loop(0, blocks)
    def _(block):
        adj_spec[block] = forward(rows_ref[2, rows_at(block), :])
        lag_spec[block] = jnp.zeros((double, channels), jnp.float32)

    filt_spec[0] = adj_spec[0]

    @pl.loop(1, blocks)
    def _(block):
        filt_spec[block, :block_len] = (
            adj_spec[block, :block_len] - sign * adj_spec[block - 1, block_len:]
        )
        filt_spec[block, block_len:] = (
            adj_spec[block, block_len:] + sign * adj_spec[block - 1, :block_len]
        )

    conv_acc[...] = jnp.zeros_like(conv_acc)
    adj_acc[...] = jnp.zeros_like(adj_acc)

    def doc_work(doc, start):
        length = lengths_ref[0, doc]
        end = start + length
        low_block = start // block_len
        high_block = jnp.where(length > 0, (end + block_len - 1) // block_len, low_block)

        def keep(block):
            pos = row_id + block * block_len
            return (pos >= start) & (pos < end)

        @pl.loop(low_block, high_block)
        def _(block):
            kept = keep(block)

            def masked(which):
                rows = rows_ref[which, rows_at(block), :].astype(jnp.float32)
                return jnp.where(kept, rows, 0.0).astype(jnp.bfloat16)

            in_spec[block] = forward(masked(0))
            wt_spec[block] = forward(masked(1))
            conv_spec[block] = jnp.zeros((double, channels), jnp.float32)
            adj_spec[block] = jnp.zeros((double, channels), jnp.float32)

        @pl.loop(low_block, high_block)
        def _(target):
            @pl.loop(low_block, target + 1)
            def _(source):
                lag = target - source
                for base in range(0, block_len, chunk):
                    re = pl.ds(base, chunk)
                    im = pl.ds(base + block_len, chunk)
                    filt_re, filt_im = filt_spec[lag, re], filt_spec[lag, im]
                    in_re, in_im = in_spec[source, re], in_spec[source, im]
                    wt_re, wt_im = wt_spec[target, re], wt_spec[target, im]
                    conv_spec[target, re] += filt_re * in_re - filt_im * in_im
                    conv_spec[target, im] += filt_re * in_im + filt_im * in_re
                    adj_spec[source, re] += filt_re * wt_re + filt_im * wt_im
                    adj_spec[source, im] += filt_re * wt_im - filt_im * wt_re
                    lag_spec[lag, re] += wt_re * in_re + wt_im * in_im
                    lag_spec[lag, im] += wt_im * in_re - wt_re * in_im

        @pl.loop(low_block, high_block)
        def _(block):
            kept = keep(block)
            conv_acc[rows_at(block), :] += jnp.where(kept, inverse(conv_spec[block]), 0.0)
            adj_acc[rows_at(block), :] += jnp.where(kept, inverse(adj_spec[block]), 0.0)

        return end

    lax.fori_loop(0, docs, doc_work, jnp.int32(0))
    conv_ref[0] = conv_acc[...].astype(jnp.bfloat16)
    conv_ref[1] = adj_acc[...].astype(jnp.bfloat16)

    @pl.loop(0, blocks - 1)
    def _(block):
        real = lag_spec[block, :block_len] + sign * lag_spec[block + 1, block_len:]
        imag = lag_spec[block, block_len:] - sign * lag_spec[block + 1, :block_len]
        lag_ref[rows_at(block), :] = inverse(jnp.concatenate([real, imag], axis=0))

    lag_ref[rows_at(blocks - 1), :] = inverse(lag_spec[blocks - 1])


def local_conv(lengths, rows, block_len):
    _, seq, channels = rows.shape
    blocks = seq // block_len
    fwd_table, inv_table = tables(block_len)
    spec = pltpu.VMEM((blocks, 2 * block_len, channels), jnp.float32)
    vmem = pl.BlockSpec(memory_space=pltpu.VMEM)
    return pl.pallas_call(
        conv_kernel,
        out_shape=(
            jax.ShapeDtypeStruct((2, seq, channels), jnp.bfloat16),
            jax.ShapeDtypeStruct((seq, channels), jnp.float32),
        ),
        in_specs=[pl.BlockSpec(memory_space=pltpu.SMEM), vmem, vmem, vmem],
        out_specs=(vmem, vmem),
        scratch_shapes=[spec] * 6 + [pltpu.VMEM((seq, channels), jnp.float32)] * 2,
        compiler_params=pltpu.CompilerParams(vmem_limit_bytes=40 * 1024 * 1024),
    )(lengths, rows, jnp.asarray(fwd_table), jnp.asarray(inv_table))


def body(queries, keys, values, cotangent, doc_lengths, filter_taps):
    block_len = queries.shape[1]
    ctx_size = lax.axis_size("ctx")
    dp_size = lax.axis_size("dp")
    ratio = ctx_size // dp_size
    ctx_rank = lax.axis_index("ctx")
    query_f = queries[0].astype(jnp.float32)
    key_f = keys[0].astype(jnp.float32)
    value_f = values[0].astype(jnp.float32)
    cot_f = cotangent[0].astype(jnp.float32)
    gated = (key_f * value_f).astype(jnp.bfloat16)
    weighted = (cot_f * query_f).astype(jnp.bfloat16)
    packed = jnp.stack([gated, weighted, filter_taps.astype(jnp.bfloat16)])
    rows = lax.all_to_all(packed, "ctx", split_axis=2, concat_axis=1, tiled=True)
    both, lags = local_conv(doc_lengths, rows, block_len)
    back = lax.all_to_all(both, "ctx", split_axis=1, concat_axis=2, tiled=True)
    lag_share = lax.psum_scatter(lags, "dp", scatter_dimension=0, tiled=True)
    lag_share = lag_share.reshape(ratio, block_len, -1)
    arrived = []
    for step in range(ratio):
        pairs = [
            (d * ctx_size + c, (c // ratio) * ctx_size + ratio * d + (c + step) % ratio)
            for d in range(dp_size)
            for c in range(ctx_size)
        ]
        piece = lax.dynamic_index_in_dim(lag_share, (ctx_rank + step) % ratio, 0, keepdims=False)
        arrived.append(lax.ppermute(piece, ("dp", "ctx"), pairs))
    arrived = jnp.stack(arrived)
    grad_filter = jnp.concatenate(
        [
            lax.dynamic_index_in_dim(arrived, (ctx_rank - m) % ratio, 0, keepdims=False)
            for m in range(ratio)
        ],
        axis=1,
    )
    conv_rows = back[0].astype(jnp.float32)
    adj_rows = back[1].astype(jnp.float32)
    hyena_out = (query_f * conv_rows).astype(jnp.bfloat16)
    grad_queries = (cot_f * conv_rows).astype(jnp.bfloat16)
    grad_keys = (adj_rows * value_f).astype(jnp.bfloat16)
    grad_values = (adj_rows * key_f).astype(jnp.bfloat16)
    return (hyena_out[None], grad_queries[None], grad_keys[None], grad_values[None], grad_filter)


def solution(mesh):
    in_specs = (
        P("dp", "ctx", None),
        P("dp", "ctx", None),
        P("dp", "ctx", None),
        P("dp", "ctx", None),
        P("dp", None),
        P("ctx", None),
    )
    out_specs = (
        P("dp", "ctx", None),
        P("dp", "ctx", None),
        P("dp", "ctx", None),
        P("dp", "ctx", None),
        P("ctx", "dp"),
    )
    return jax.shard_map(body, mesh=mesh, in_specs=in_specs, out_specs=out_specs, check_vma=False)
```

time: 782 us -> 148 us (0.19)
  the two profiles are of different devices: /device:TPU:3 before, /device:TPU:2 now
where the time goes in v1:
time: 148 us; the launch traced here: 147 us
  blocking collectives  54 us (36%)
  waiting for transfers between devices  35.9 us (24%)
  between operations  14.2 us (10%)
  Pallas kernels  13.8 us (9%)
  starting transfers between devices  10.3 us (7%)
  local copies, waits for them, and re-layouts  10.1 us (7%)
  other arithmetic  8.87 us (6%)
    all_to_all x1, blocking collectives, body(): lax.all_to_all(packed, 'ctx', split_axis=2, concat_axis=1, tiled=True)  54 us
    all_to_all x1, waiting for transfers between devices, body(): back = lax.all_to_all(both, 'ctx', split_axis=1, concat_axis=2, tiled=True)  25.1 us
    pallas_call x1, Pallas kernels, local_conv(): pl.pallas_call(conv_kernel, out_shape=(jax.ShapeDtypeStruct((2, seq, chan...  13.8 us
    ppermute x2, waiting for transfers between devices, body(): arrived.append(lax.ppermute(piece, ('dp', 'ctx'), pairs))  10.1 us
    ppermute x2, starting transfers between devices, body(): arrived.append(lax.ppermute(piece, ('dp', 'ctx'), pairs))  6.67 us
    all_to_all x1, starting transfers between devices, body(): back = lax.all_to_all(both, 'ctx', split_axis=1, concat_axis=2, tiled=True)  3.59 us
    another operation x1, local copies, waits for them, and re-layouts, body(): packed = jnp.stack([gated, weighted, filter_taps.astype(jnp.bfloat16)])  3.01 us
  transfers between devices with their start and end apart: 4, of which 3 were waited for; matrix products, arithmetic and copies ran while one was open for 3% of the time, Pallas kernels for 0%

profile of v1, /device:TPU:2, one launch (start us, length us, event | category | flops | bytes accessed | tf_op | source)
XLA Modules:
  0.0 147.2 jit_solution(2017049640060962566)
XLA Ops:
  7.2 0.0 copy-start.5
  7.2 0.0 copy-start.3
  7.2 0.0 copy-start.4
  7.2 1.4 convert_bitcast_fusion
  8.6 0.0 copy-done.5
  8.6 0.1 copy-done.3
  8.7 0.2 copy-done.4
  8.8 1.4 fusion.2
  10.3 1.4 pad_maximum_fusion
  11.6 3.0 %copy.28 = bf16[3,128,2048]{1,0,2:T(4,128)(2,1)S(1)} copy(bf16[3,128,2048]{2,1,0:T(8,128)(2,1)} %pad_maximum_fusion) | data formatting | bytes 3145728 | tf_op jit(solution)/shard_map/stack | solution.py:172
  14.6 54.0 %all_to_all.33 = bf16[3,128,2048]{1,0,2:T(4,128)(2,1)} all-to-all(bf16[3,128,2048]{1,0,2:T(4,128)(2,1)S(1)} %copy.28), channel_id=1, replica_groups=mesh['dp'=4,'ctx'=8] {'ctx'}, dimensions={2} | all-to-all | bytes 3145728 | tf_op jit(solution)/shard_map/all_to_all | solution.py:173
  68.6 0.0 copy-start
  68.6 0.0 copy-start.1
  68.6 0.0 copy-start.2
  68.6 2.9 %copy.29 = bf16[3,128,8,256]{3,1,2,0:T(8,128)(2,1)S(1)} copy(bf16[3,128,8,256]{1,0,3,2:T(4,128)(2,1)} %bitcast.26) | data formatting | bytes 3145728 | tf_op jit(solution)/shard_map/all_to_all | solution.py:173
  71.5 0.0 copy-done
  71.6 0.0 copy-done.1
  71.6 0.0 copy-done.2
  71.6 13.8 %shard_map.119 = (bf16[2,1024,256]{2,1,0:T(8,128)(2,1)S(1)}, f32[1024,256]{1,0:T(8,128)}) custom-call(s32[1,4]{1,0:T(1,128)S(1)} %copy-done.2, bf16[3,1024,256]{2,1,0:T(8,128)(2,1)S(1)} %bitcast.25, bf16[256,256]{1,0:T(8,128)(2,1)S(1)} %copy-done.1, bf16[128,768]{1,0:T(8,128)(2,1)S(1)} %copy-done), custom_call_target="tpu_custom_call" | custom-call | tf_op jit(solution)/shard_map/pallas_call | solution.py:147
  85.3 2.1 %copy.30 = bf16[2,1024,256]{2,0,1:T(2,128)(2,1)} copy(bf16[2,1024,256]{2,1,0:T(8,128)(2,1)S(1)} %get-tuple-element.7) | data formatting | bytes 2097152 | tf_op jit(solution)/shard_map/pallas_call | solution.py:147
  87.4 3.6 %all-to-all-start.1 = ((bf16[2,1024,256]{2,0,1:T(2,128)(2,1)}), bf16[2,1024,256]{2,0,1:T(2,128)(2,1)S(1)}, u32[]{:S(2)}, u32[]{:S(2)}) async-start(bf16[2,1024,256]{2,0,1:T(2,128)(2,1)} %copy.30), calls=%async_computation.1 | async-start | bytes 2097152 | tf_op jit(solution)/shard_map/all_to_all | solution.py:175
  91.0 0.0 reduce-scatter.2.cloned.1.call-start
  91.0 0.7 reduce-scatter.2.cloned.1.call-update
  91.8 25.1 %all-to-all-done.1 = bf16[2,1024,256]{2,0,1:T(2,128)(2,1)S(1)} async-done(((bf16[2,1024,256]{2,0,1:T(2,128)(2,1)}), bf16[2,1024,256]{2,0,1:T(2,128)(2,1)S(1)}, u32[]{:S(2)}, u32[]{:S(2)}) %all-to-all-start.1) | async-done | bytes 1048608 | tf_op jit(solution)/shard_map/all_to_all | solution.py:175
  116.9 0.6 copy.33
  117.5 0.2 slice_convert_fusion
  117.7 0.2 reshape.44
  117.8 0.2 reshape.45
  118.0 0.0 copy-start.6
  118.0 0.0 copy-start.7
  118.0 2.5 %fusion.5 = (bf16[1,128,2048]{2,1,0:T(8,128)(2,1)}, bf16[1,128,2048]{2,1,0:T(8,128)(2,1)}) fusion(f32[1,128,2048]{2,1,0:T(8,128)S(1)} %reshape.44, bf16[1,128,2048]{2,1,0:T(8,128)(2,1)} %param.11, bf16[1,128,2048]{2,1,0:T(8,128)(2,1)} %param.8), kind=kLoop, calls=%fused_computation.12 | loop fusion | flops 1572864 | bytes 3145728 | tf_op jit(solution)/shard_map/convert_element_type | solution.py:198
  120.5 0.0 reduce-scatter.2.cloned.1.call-done
  120.5 1.0 dynamic-slice_bitcast_fusion
  121.5 4.4 %collective-permute-start = (f32[128,256]{1,0:T(8,128)S(1)}, f32[128,256]{1,0:T(8,128)S(1)}, u32[]{:S(2)}, u32[]{:S(2)}) collective-permute-start(f32[128,256]{1,0:T(8,128)S(1)} %get-tuple-element.23), channel_id=1, source_target_pairs={{0,0},{1,1},{2,8},{3,9},{4,16},{5,17},{6,24},{7,25},{8,2},{9,3},{1... | collective-permute-start | bytes 393224 | tf_op jit(solution)/shard_map/ppermute | solution.py:186
  125.9 2.3 %collective-permute-start.1 = (f32[128,256]{1,0:T(8,128)S(1)}, f32[128,256]{1,0:T(8,128)S(1)}, u32[]{:S(2)}, u32[]{:S(2)}) collective-permute-start(f32[128,256]{1,0:T(8,128)S(1)} %get-tuple-element.22), channel_id=1, source_target_pairs={{0,1},{1,0},{2,9},{3,8},{4,17},{5,16},{6,25},{7,24},{8,3},{9,2},{1... | collective-permute-start | bytes 393224 | tf_op jit(solution)/shard_map/ppermute | solution.py:186
  128.2 0.0 copy-done.6
  128.2 0.0 copy-done.7
  128.2 1.2 fusion.1
  129.4 6.9 %collective-permute-done = f32[128,256]{1,0:T(8,128)S(1)} collective-permute-done((f32[128,256]{1,0:T(8,128)S(1)}, f32[128,256]{1,0:T(8,128)S(1)}, u32[]{:S(2)}, u32[]{:S(2)}) %collective-permute-start) | collective-permute-done | bytes 131104 | tf_op jit(solution)/shard_map/ppermute | solution.py:186
  136.3 3.2 %collective-permute-done.1 = f32[128,256]{1,0:T(8,128)S(1)} collective-permute-done((f32[128,256]{1,0:T(8,128)S(1)}, f32[128,256]{1,0:T(8,128)S(1)}, u32[]{:S(2)}, u32[]{:S(2)}) %collective-permute-start.1) | collective-permute-done | bytes 131104 | tf_op jit(solution)/shard_map/ppermute | solution.py:186
  139.6 0.1 fusion.9
  139.6 0.7 pad_maximum_fusion.1
Async XLA Ops:
  7.2 1.4 copy-start.5
  7.2 1.5 %copy-start.3 = (bf16[1,128,2048]{2,1,0:T(8,128)(2,1)S(1)}, bf16[1,128,2048]{2,1,0:T(8,128)(2,1)}, u32[]{:S(2)}) copy-start(bf16[1,128,2048]{2,1,0:T(8,128)(2,1)} %param.8) | copy-start | bytes 1572868
  7.2 1.7 %copy-start.4 = (bf16[1,128,2048]{2,1,0:T(8,128)(2,1)S(1)}, bf16[1,128,2048]{2,1,0:T(8,128)(2,1)}, u32[]{:S(2)}) copy-start(bf16[1,128,2048]{2,1,0:T(8,128)(2,1)} %param.11) | copy-start | bytes 1572868
  68.6 2.9 %copy-start = (bf16[128,768]{1,0:T(8,128)(2,1)S(1)}, bf16[128,768]{1,0:T(8,128)(2,1)}, u32[]{:S(2)}) copy-start(bf16[128,768]{1,0:T(8,128)(2,1)} %constant.45.clone.inv_ref) | copy-start | bytes 589828
  68.6 2.9 %copy-start.1 = (bf16[256,256]{1,0:T(8,128)(2,1)S(1)}, bf16[256,256]{1,0:T(8,128)(2,1)}, u32[]{:S(2)}) copy-start(bf16[256,256]{1,0:T(8,128)(2,1)} %constant.44.clone.fwd_ref) | copy-start | bytes 393220
  68.6 2.9 %copy-start.2 = (s32[1,4]{1,0:T(1,128)S(1)}, s32[1,4]{1,0:T(1,128)}, u32[]{:S(2)}) copy-start(s32[1,4]{1,0:T(1,128)} %lengths_ref.1) | copy-start | bytes 52
  87.4 29.5 %all-to-all-start.1 = ((bf16[2,1024,256]{2,0,1:T(2,128)(2,1)}), bf16[2,1024,256]{2,0,1:T(2,128)(2,1)S(1)}, u32[]{:S(2)}, u32[]{:S(2)}) async-start(bf16[2,1024,256]{2,0,1:T(2,128)(2,1)} %copy.30), calls=%async_computation.1 | async-start | bytes 2097152 | tf_op jit(solution)/shard_map/all_to_all | solution.py:175
  91.0 29.6 %reduce-scatter.2.cloned.1.call-start = ((), (), s32[]{:S(2)}) async-start(), calls=%async_computation.3 | async-start | bytes 1310720 | tf_op jit(solution)/shard_map/reduce_scatter | solution.py:176
  118.0 10.2 %copy-start.6 = (bf16[1,128,2048]{2,1,0:T(8,128)(2,1)S(1)}, bf16[1,128,2048]{2,1,0:T(8,128)(2,1)}, u32[]{:S(2)}) copy-start(bf16[1,128,2048]{2,1,0:T(8,128)(2,1)} %param.10) | copy-start | bytes 1572868
  118.0 10.2 %copy-start.7 = (bf16[1,128,2048]{2,1,0:T(8,128)(2,1)S(1)}, bf16[1,128,2048]{2,1,0:T(8,128)(2,1)}, u32[]{:S(2)}) copy-start(bf16[1,128,2048]{2,1,0:T(8,128)(2,1)} %param.9) | copy-start | bytes 1572868
  121.5 14.8 %collective-permute-start = (f32[128,256]{1,0:T(8,128)S(1)}, f32[128,256]{1,0:T(8,128)S(1)}, u32[]{:S(2)}, u32[]{:S(2)}) collective-permute-start(f32[128,256]{1,0:T(8,128)S(1)} %get-tuple-element.23), channel_id=1, source_target_pairs={{0,0},{1,1},{2,8},{3,9},{4,16},{5,17},{6,24},{7,25},{8,2},{9,3},{1... | collective-permute-start | bytes 393224 | tf_op jit(solution)/shard_map/ppermute | solution.py:186
  125.9 13.6 %collective-permute-start.1 = (f32[128,256]{1,0:T(8,128)S(1)}, f32[128,256]{1,0:T(8,128)S(1)}, u32[]{:S(2)}, u32[]{:S(2)}) collective-permute-start(f32[128,256]{1,0:T(8,128)S(1)} %get-tuple-element.22), channel_id=1, source_target_pairs={{0,1},{1,0},{2,9},{3,8},{4,17},{5,16},{6,25},{7,24},{8,3},{9,2},{1... | collective-permute-start | bytes 393224 | tf_op jit(solution)/shard_map/ppermute | solution.py:186
Sparse Core Ops, SparseCore 0:
  94.3 25.1 reduce-scatter.1

commit v2 on v1

--- a/solution.py
+++ b/solution.py
@@ -31,7 +31,7 @@
 
 
 def conv_kernel(
-    lengths_ref, rows_ref, fwd_ref, inv_ref, conv_ref, lag_ref,
+    lengths_ref, rows_ref, taps_ref, fwd_ref, inv_ref, conv_ref, lag_ref,
     in_spec, wt_spec, filt_spec, conv_spec, adj_spec, lag_spec, conv_acc, adj_acc,
 ):
     blocks, double, channels = in_spec.shape
@@ -59,7 +59,8 @@
 
     @pl.loop(0, blocks)
     def _(block):
-        adj_spec[block] = forward(rows_ref[2, rows_at(block), :])
+        taps = [taps_ref[part, block] for part in range(taps_ref.shape[0])]
+        adj_spec[block] = forward(jnp.concatenate(taps, axis=0))
         lag_spec[block] = jnp.zeros((double, channels), jnp.float32)
 
     filt_spec[0] = adj_spec[0]
@@ -91,7 +92,7 @@
             kept = keep(block)
 
             def masked(which):
-                rows = rows_ref[which, rows_at(block), :].astype(jnp.float32)
+                rows = rows_ref[block, which].astype(jnp.float32)
                 return jnp.where(kept, rows, 0.0).astype(jnp.bfloat16)
 
             in_spec[block] = forward(masked(0))
@@ -126,8 +127,11 @@
         return end
 
     lax.fori_loop(0, docs, doc_work, jnp.int32(0))
-    conv_ref[0] = conv_acc[...].astype(jnp.bfloat16)
-    conv_ref[1] = adj_acc[...].astype(jnp.bfloat16)
+
+    @pl.loop(0, blocks)
+    def _(block):
+        conv_ref[block, 0] = conv_acc[rows_at(block), :].astype(jnp.bfloat16)
+        conv_ref[block, 1] = adj_acc[rows_at(block), :].astype(jnp.bfloat16)
 
     @pl.loop(0, blocks - 1)
     def _(block):
@@ -138,41 +142,83 @@
     lag_ref[rows_at(blocks - 1), :] = inverse(lag_spec[blocks - 1])
 
 
-def local_conv(lengths, rows, block_len):
-    _, seq, channels = rows.shape
-    blocks = seq // block_len
+def local_conv(lengths, rows, taps):
+    blocks, _, block_len, channels = rows.shape
+    seq = blocks * block_len
     fwd_table, inv_table = tables(block_len)
     spec = pltpu.VMEM((blocks, 2 * block_len, channels), jnp.float32)
     vmem = pl.BlockSpec(memory_space=pltpu.VMEM)
     return pl.pallas_call(
         conv_kernel,
         out_shape=(
-            jax.ShapeDtypeStruct((2, seq, channels), jnp.bfloat16),
+            jax.ShapeDtypeStruct(rows.shape, jnp.bfloat16),
             jax.ShapeDtypeStruct((seq, channels), jnp.float32),
         ),
-        in_specs=[pl.BlockSpec(memory_space=pltpu.SMEM), vmem, vmem, vmem],
+        in_specs=[pl.BlockSpec(memory_space=pltpu.SMEM), vmem, vmem, vmem, vmem],
         out_specs=(vmem, vmem),
         scratch_shapes=[spec] * 6 + [pltpu.VMEM((seq, channels), jnp.float32)] * 2,
         compiler_params=pltpu.CompilerParams(vmem_limit_bytes=40 * 1024 * 1024),
-    )(lengths, rows, jnp.asarray(fwd_table), jnp.asarray(inv_table))
+    )(lengths, rows, taps, jnp.asarray(fwd_table), jnp.asarray(inv_table))
+
+
+GROUP = 2
+
+
+def gate_kernel(query_ref, key_ref, value_ref, cot_ref, out_ref):
+    channels = out_ref.shape[3]
+    for part in range(GROUP):
+        cols = pl.ds(part * channels, channels)
+
+        def load(ref):
+            return ref[0, :, cols].astype(jnp.float32)
+
+        out_ref[part, 0] = (load(key_ref) * load(value_ref)).astype(jnp.bfloat16)
+        out_ref[part, 1] = (load(cot_ref) * load(query_ref)).astype(jnp.bfloat16)
+
+
+def finish_kernel(
+    back_ref, query_ref, key_ref, value_ref, cot_ref, out_ref, dquery_ref, dkey_ref, dvalue_ref
+):
+    channels = back_ref.shape[3]
+    for part in range(GROUP):
+        cols = pl.ds(part * channels, channels)
+
+        def load(ref):
+            return ref[0, :, cols].astype(jnp.float32)
+
+        conv_rows = back_ref[part, 0].astype(jnp.float32)
+        adj_rows = back_ref[part, 1].astype(jnp.float32)
+        out_ref[0, :, cols] = (load(query_ref) * conv_rows).astype(jnp.bfloat16)
+        dquery_ref[0, :, cols] = (load(cot_ref) * conv_rows).astype(jnp.bfloat16)
+        dkey_ref[0, :, cols] = (adj_rows * load(value_ref)).astype(jnp.bfloat16)
+        dvalue_ref[0, :, cols] = (adj_rows * load(key_ref)).astype(jnp.bfloat16)
 
 
 def body(queries, keys, values, cotangent, doc_lengths, filter_taps):
-    block_len = queries.shape[1]
+    block_len, width = queries.shape[1:]
     ctx_size = lax.axis_size("ctx")
     dp_size = lax.axis_size("dp")
     ratio = ctx_size // dp_size
     ctx_rank = lax.axis_index("ctx")
-    query_f = queries[0].astype(jnp.float32)
-    key_f = keys[0].astype(jnp.float32)
-    value_f = values[0].astype(jnp.float32)
-    cot_f = cotangent[0].astype(jnp.float32)
-    gated = (key_f * value_f).astype(jnp.bfloat16)
-    weighted = (cot_f * query_f).astype(jnp.bfloat16)
-    packed = jnp.stack([gated, weighted, filter_taps.astype(jnp.bfloat16)])
-    rows = lax.all_to_all(packed, "ctx", split_axis=2, concat_axis=1, tiled=True)
-    both, lags = local_conv(doc_lengths, rows, block_len)
-    back = lax.all_to_all(both, "ctx", split_axis=1, concat_axis=2, tiled=True)
+    channels = width // ctx_size
+    wide = pl.BlockSpec((1, block_len, GROUP * channels), lambda i: (0, 0, i))
+    packed_spec = pl.BlockSpec((GROUP, 2, block_len, channels), lambda i: (i, 0, 0, 0))
+    share = block_len // dp_size
+    piece = lax.dynamic_slice_in_dim(filter_taps, lax.axis_index("dp") * share, share, 0)
+    piece = piece.astype(jnp.bfloat16).reshape(share, ctx_size, channels).transpose(1, 0, 2)
+    piece = lax.all_to_all(piece, "ctx", split_axis=0, concat_axis=0, tiled=True)
+    packed = pl.pallas_call(
+        gate_kernel,
+        grid=(ctx_size // GROUP,),
+        out_shape=jax.ShapeDtypeStruct((ctx_size, 2, block_len, channels), jnp.bfloat16),
+        in_specs=[wide] * 4,
+        out_specs=packed_spec,
+    )(queries, keys, values, cotangent)
+    packed, piece = lax.optimization_barrier((packed, piece))
+    taps = lax.all_gather(piece, "dp", axis=0, tiled=False)
+    rows = lax.all_to_all(packed, "ctx", split_axis=0, concat_axis=0, tiled=True)
+    both, lags = local_conv(doc_lengths, rows, taps)
+    back = lax.all_to_all(both, "ctx", split_axis=0, concat_axis=0, tiled=True)
     lag_share = lax.psum_scatter(lags, "dp", scatter_dimension=0, tiled=True)
     lag_share = lag_share.reshape(ratio, block_len, -1)
     arrived = []
@@ -192,13 +238,14 @@
         ],
         axis=1,
     )
-    conv_rows = back[0].astype(jnp.float32)
-    adj_rows = back[1].astype(jnp.float32)
-    hyena_out = (query_f * conv_rows).astype(jnp.bfloat16)
-    grad_queries = (cot_f * conv_rows).astype(jnp.bfloat16)
-    grad_keys = (adj_rows * value_f).astype(jnp.bfloat16)
-    grad_values = (adj_rows * key_f).astype(jnp.bfloat16)
-    return (hyena_out[None], grad_queries[None], grad_keys[None], grad_values[None], grad_filter)
+    outs = pl.pallas_call(
+        finish_kernel,
+        grid=(ctx_size // GROUP,),
+        out_shape=(jax.ShapeDtypeStruct(queries.shape, jnp.bfloat16),) * 4,
+        in_specs=[packed_spec] + [wide] * 4,
+        out_specs=(wide,) * 4,
+    )(back, queries, keys, values, cotangent)
+    return (*outs, grad_filter)
 
 
 def solution(mesh):

time: 148 us -> 115 us (0.78)
  blocking collectives: 54 us -> 6.64 us
  waiting for transfers between devices: 35.9 us -> 47.3 us
  starting transfers between devices: 10.3 us -> 19.9 us
  other arithmetic: 8.87 us -> 0.79 us
  Pallas kernels: 13.8 us -> 20.8 us
  local copies, waits for them, and re-layouts: 10.1 us -> 4.91 us
    all_to_all x1 -> x0, blocking collectives: 54 us -> none  [body(): lax.all_to_all(packed, 'ctx', split_axis=2, concat_axis=1, tiled=True)]
    reduce_scatter x1, waiting for transfers between devices: 0.01 us -> 19.7 us  [body(): lag_share = lax.psum_scatter(lags, 'dp', scatter_dimension=0, tiled=True)]
    all_to_all x1 -> x3, starting transfers between devices: 3.59 us -> 13 us  [the longest x1 5.83 us: body(): lax.all_to_all(piece, 'ctx', split_axis=0, concat_axis=0, tiled=True)]
    pallas_call x1 -> x3, Pallas kernels: 13.8 us -> 20.8 us  [the longest x1 13.1 us: local_conv(): pl.pallas_call(conv_kernel, out_shape=(jax.ShapeDtypeStruct(rows.shape, j...]
    all_gather x0 -> x1, blocking collectives: none -> 6.64 us  [body(): taps = lax.all_gather(piece, 'dp', axis=0, tiled=False)]
    convert_element_type x4 -> x0, other arithmetic: 5.34 us -> none  [the longest x1 2.52 us: body(): grad_queries = (cot_f * conv_rows).astype(jnp.bfloat16)]
    ppermute x2, waiting for transfers between devices: 10.1 us -> 5.92 us  [body(): arrived.append(lax.ppermute(piece, ('dp', 'ctx'), pairs))]
    all_to_all x2 -> x0, local copies, waits for them, and re-layouts: 3.49 us -> none  [the longest x1 2.91 us: body(): lax.all_to_all(packed, 'ctx', split_axis=2, concat_axis=1, tiled=True)]
  transfers between devices with their start and end apart: 4 -> 6, of which waited for: 3 -> 5; matrix products, arithmetic and copies ran while one was open for 3% -> 1% of each run, Pallas kernels for 0% -> 7%
where the time goes in v2:
time: 115 us
  waiting for transfers between devices  47.3 us (41%)
  Pallas kernels  20.8 us (18%)
  starting transfers between devices  19.9 us (17%)
  between operations  14.2 us (12%)
  blocking collectives  6.64 us (6%)
  local copies, waits for them, and re-layouts  4.91 us (4%)
    reduce_scatter x1, waiting for transfers between devices, body(): lag_share = lax.psum_scatter(lags, 'dp', scatter_dimension=0, tiled=True)  19.7 us
    all_to_all x1, waiting for transfers between devices, body(): lax.all_to_all(packed, 'ctx', split_axis=0, concat_axis=0, tiled=True)  18 us
    pallas_call x1, Pallas kernels, local_conv(): pl.pallas_call(conv_kernel, out_shape=(jax.ShapeDtypeStruct(rows.shape, j...  13.1 us
    ppermute x2, starting transfers between devices, body(): arrived.append(lax.ppermute(piece, ('dp', 'ctx'), pairs))  6.95 us
    all_gather x1, blocking collectives, body(): taps = lax.all_gather(piece, 'dp', axis=0, tiled=False)  6.64 us
    ppermute x2, waiting for transfers between devices, body(): arrived.append(lax.ppermute(piece, ('dp', 'ctx'), pairs))  5.92 us
    all_to_all x1, starting transfers between devices, body(): lax.all_to_all(piece, 'ctx', split_axis=0, concat_axis=0, tiled=True)  5.83 us
    pallas_call x1, Pallas kernels, body(): pl.pallas_call(finish_kernel, grid=(ctx_size // GROUP,), out_shape=(jax.S...  3.98 us
  transfers between devices with their start and end apart: 6, of which 5 were waited for; matrix products, arithmetic and copies ran while one was open for 1% of the time, Pallas kernels for 7%

profile of v2, /device:TPU:2, one launch (start us, length us, event | category | flops | bytes accessed | tf_op | source)
XLA Modules:
  0.0 114.5 jit_solution(2075017463806179385)
XLA Ops:
  7.2 0.0 copy-start
  7.2 1.2 %copy-done = f32[128,2048]{1,0:T(8,128)S(1)} copy-done((f32[128,2048]{1,0:T(8,128)S(1)}, f32[128,2048]{1,0:T(8,128)}, u32[]{:S(2)}) %copy-start) | copy-done | bytes 1048600
  8.4 0.7 copy.15
  9.1 5.8 %all-to-all-start = ((bf16[8,32,256]{2,1,0:T(8,128)(2,1)}), bf16[8,32,256]{2,1,0:T(8,128)(2,1)S(1)}, u32[]{:S(2)}, u32[]{:S(2)}) async-start(bf16[8,32,256]{2,1,0:T(8,128)(2,1)} %copy.15), calls=%async_computation | async-start | bytes 262144 | tf_op jit(solution)/shard_map/all_to_all | solution.py:209
  15.0 3.7 %shard_map.119 = bf16[8,2,128,256]{3,2,1,0:T(8,128)(2,1)} custom-call(bf16[1,128,2048]{2,1,0:T(8,128)(2,1)} %query_ref.3, bf16[1,128,2048]{2,1,0:T(8,128)(2,1)} %key_ref.3, bf16[1,128,2048]{2,1,0:T(8,128)(2,1)} %value_ref.3, bf16[1,128,2048]{2,1,0:T(8,128)(2,1)} %cot_ref.3), custom_call_target="tpu_custom_call" | custom-call | tf_op jit(solution)/shard_map/pallas_call | solution.py:210
  18.7 3.6 %all-to-all-done = bf16[8,32,256]{2,1,0:T(8,128)(2,1)S(1)} async-done(((bf16[8,32,256]{2,1,0:T(8,128)(2,1)}), bf16[8,32,256]{2,1,0:T(8,128)(2,1)S(1)}, u32[]{:S(2)}, u32[]{:S(2)}) %all-to-all-start) | async-done | bytes 131104 | tf_op jit(solution)/shard_map/all_to_all | solution.py:209
  22.3 3.6 %all-to-all-start.1 = ((bf16[8,2,128,256]{3,2,1,0:T(8,128)(2,1)}), bf16[8,2,128,256]{3,2,1,0:T(8,128)(2,1)S(1)}, u32[]{:S(2)}, u32[]{:S(2)}) async-start(bf16[8,2,128,256]{3,2,1,0:T(8,128)(2,1)} %shard_map.119), calls=%async_computation.1 | async-start | bytes 2097152 | tf_op jit(solution)/shard_map/all_to_all | solution.py:219
  25.9 0.0 copy-start.2
  25.9 0.0 copy-start.3
  25.9 0.0 reduce-scatter.2.cloned.1.call-start
  25.9 6.6 %all-gather = bf16[32,32,256]{2,1,0:T(8,128)(2,1)S(1)} all-gather(bf16[8,32,256]{2,1,0:T(8,128)(2,1)S(1)} %all-to-all-done), channel_id=2, replica_groups=mesh['dp'=4,'ctx'=8] {'dp'}, dimensions={0}, use_global_device_ids=true | all-gather | bytes 655360 | tf_op jit(solution)/shard_map/all_gather | solution.py:218
  32.6 0.0 copy-start.4
  32.6 18.0 %all-to-all-done.1.rows_ref = bf16[8,2,128,256]{3,2,1,0:T(8,128)(2,1)S(1)} async-done(((bf16[8,2,128,256]{3,2,1,0:T(8,128)(2,1)}), bf16[8,2,128,256]{3,2,1,0:T(8,128)(2,1)S(1)}, u32[]{:S(2)}, u32[]{:S(2)}) %all-to-all-start.1) | async-done | bytes 1048608 | tf_op jit(solution)/shard_map/all_to_all | solution.py:219
  50.6 0.0 copy-done.2
  50.6 0.0 copy-done.3
  50.6 0.0 copy-done.4
  50.6 13.1 %shard_map.120 = (bf16[8,2,128,256]{3,2,1,0:T(8,128)(2,1)}, f32[1024,256]{1,0:T(8,128)S(1)}) custom-call(s32[1,4]{1,0:T(1,128)S(1)} %copy-done.4, bf16[8,2,128,256]{3,2,1,0:T(8,128)(2,1)S(1)} %all-to-all-done.1.rows_ref, bf16[4,8,32,256]{3,2,1,0:T(8,128)(2,1)S(1)} %bitcast.16, bf16[256,256]{1,0:T(8,128)(2,1)S(1)} %copy-done.3, bf16[128,768]{1,0:T(8,128)(2,1)S(1)} %copy-done.2), custom_call_target="tpu_custom_call" | custom-call | tf_op jit(solution)/shard_map/pallas_call | solution.py:151
  63.8 0.0 copy-start.1
  63.8 1.0 copy-done.1
  64.8 0.0 reduce-scatter.2.cloned.1.call-update
  64.8 3.6 %all-to-all-start.2 = ((bf16[8,2,128,256]{3,2,1,0:T(8,128)(2,1)}), bf16[8,2,128,256]{3,2,1,0:T(8,128)(2,1)S(1)}, u32[]{:S(2)}, u32[]{:S(2)}) async-start(bf16[8,2,128,256]{3,2,1,0:T(8,128)(2,1)} %get-tuple-element.15), calls=%async_computation.2 | async-start | bytes 2097152 | tf_op jit(solution)/shard_map/all_to_all | solution.py:221
  68.4 19.7 %reduce-scatter.2.cloned.1.call-done = f32[256,256]{1,0:T(8,128)} async-done(((f32[1024,256]{1,0:T(8,128)}), f32[256,256]{1,0:T(8,128)}) %reduce-scatter.2.cloned.1.call-update) | async-done | bytes 262160 | tf_op jit(solution)/shard_map/reduce_scatter | solution.py:222
  88.0 1.0 dynamic-slice_bitcast_fusion
  89.0 4.5 %collective-permute-start.1 = (f32[128,256]{1,0:T(8,128)S(1)}, f32[128,256]{1,0:T(8,128)S(1)}, u32[]{:S(2)}, u32[]{:S(2)}) collective-permute-start(f32[128,256]{1,0:T(8,128)S(1)} %get-tuple-element.23), channel_id=1, source_target_pairs={{0,1},{1,0},{2,9},{3,8},{4,17},{5,16},{6,25},{7,24},{8,3},{9,2},{1... | collective-permute-start | bytes 393224 | tf_op jit(solution)/shard_map/ppermute | solution.py:232
  93.6 2.4 %collective-permute-start = (f32[128,256]{1,0:T(8,128)S(1)}, f32[128,256]{1,0:T(8,128)S(1)}, u32[]{:S(2)}, u32[]{:S(2)}) collective-permute-start(f32[128,256]{1,0:T(8,128)S(1)} %get-tuple-element.24), channel_id=1, source_target_pairs={{0,0},{1,1},{2,8},{3,9},{4,16},{5,17},{6,24},{7,25},{8,2},{9,3},{1... | collective-permute-start | bytes 393224 | tf_op jit(solution)/shard_map/ppermute | solution.py:232
  96.0 0.0 all-to-all-done.2.back_ref
  96.0 0.0 copy-start.5
  96.0 1.0 copy-done.5
  97.0 4.0 %shard_map.121 = (bf16[1,128,2048]{2,1,0:T(8,128)(2,1)}, bf16[1,128,2048]{2,1,0:T(8,128)(2,1)}, bf16[1,128,2048]{2,1,0:T(8,128)(2,1)}, bf16[1,128,2048]{2,1,0:T(8,128)(2,1)}) custom-call(bf16[8,2,128,256]{3,2,1,0:T(8,128)(2,1)} %copy-done.5, bf16[1,128,2048]{2,1,0:T(8,128)(2,1)} %query_ref.3, bf16[1,128,2048]{2,1,0:T(8,128)(2,1)} %key_ref.3, ...), custom_call_target="tpu_custom_call" | custom-call | tf_op jit(solution)/shard_map/pallas_call | solution.py:241
  101.0 3.7 %collective-permute-done.1 = f32[128,256]{1,0:T(8,128)S(1)} collective-permute-done((f32[128,256]{1,0:T(8,128)S(1)}, f32[128,256]{1,0:T(8,128)S(1)}, u32[]{:S(2)}, u32[]{:S(2)}) %collective-permute-start.1) | collective-permute-done | bytes 131104 | tf_op jit(solution)/shard_map/ppermute | solution.py:232
  104.7 2.2 %collective-permute-done = f32[128,256]{1,0:T(8,128)S(1)} collective-permute-done((f32[128,256]{1,0:T(8,128)S(1)}, f32[128,256]{1,0:T(8,128)S(1)}, u32[]{:S(2)}, u32[]{:S(2)}) %collective-permute-start) | collective-permute-done | bytes 131104 | tf_op jit(solution)/shard_map/ppermute | solution.py:232
  106.9 0.1 fusion.3
  107.0 0.7 pad_maximum_fusion
  (2 shorter events, 0.0 us)
Async XLA Ops:
  7.2 1.2 %copy-start = (f32[128,2048]{1,0:T(8,128)S(1)}, f32[128,2048]{1,0:T(8,128)}, u32[]{:S(2)}) copy-start(f32[128,2048]{1,0:T(8,128)} %param.13) | copy-start | bytes 3145732
  9.1 13.2 %all-to-all-start = ((bf16[8,32,256]{2,1,0:T(8,128)(2,1)}), bf16[8,32,256]{2,1,0:T(8,128)(2,1)S(1)}, u32[]{:S(2)}, u32[]{:S(2)}) async-start(bf16[8,32,256]{2,1,0:T(8,128)(2,1)} %copy.15), calls=%async_computation | async-start | bytes 262144 | tf_op jit(solution)/shard_map/all_to_all | solution.py:209
  22.3 28.3 %all-to-all-start.1 = ((bf16[8,2,128,256]{3,2,1,0:T(8,128)(2,1)}), bf16[8,2,128,256]{3,2,1,0:T(8,128)(2,1)S(1)}, u32[]{:S(2)}, u32[]{:S(2)}) async-start(bf16[8,2,128,256]{3,2,1,0:T(8,128)(2,1)} %shard_map.119), calls=%async_computation.1 | async-start | bytes 2097152 | tf_op jit(solution)/shard_map/all_to_all | solution.py:219
  25.9 24.7 %copy-start.2 = (bf16[128,768]{1,0:T(8,128)(2,1)S(1)}, bf16[128,768]{1,0:T(8,128)(2,1)}, u32[]{:S(2)}) copy-start(bf16[128,768]{1,0:T(8,128)(2,1)} %constant.54.clone.inv_ref) | copy-start | bytes 589828
  25.9 24.7 %copy-start.3 = (bf16[256,256]{1,0:T(8,128)(2,1)S(1)}, bf16[256,256]{1,0:T(8,128)(2,1)}, u32[]{:S(2)}) copy-start(bf16[256,256]{1,0:T(8,128)(2,1)} %constant.53.clone.fwd_ref) | copy-start | bytes 393220
  25.9 62.2 %reduce-scatter.2.cloned.1.call-start = ((), (), s32[]{:S(2)}) async-start(), calls=%async_computation.4 | async-start | bytes 1310720 | tf_op jit(solution)/shard_map/reduce_scatter | solution.py:222
  32.6 18.0 %copy-start.4 = (s32[1,4]{1,0:T(1,128)S(1)}, s32[1,4]{1,0:T(1,128)}, u32[]{:S(2)}) copy-start(s32[1,4]{1,0:T(1,128)} %lengths_ref.1) | copy-start | bytes 52
  63.8 1.0 copy-start.1
  64.8 31.2 %all-to-all-start.2 = ((bf16[8,2,128,256]{3,2,1,0:T(8,128)(2,1)}), bf16[8,2,128,256]{3,2,1,0:T(8,128)(2,1)S(1)}, u32[]{:S(2)}, u32[]{:S(2)}) async-start(bf16[8,2,128,256]{3,2,1,0:T(8,128)(2,1)} %get-tuple-element.15), calls=%async_computation.2 | async-start | bytes 2097152 | tf_op jit(solution)/shard_map/all_to_all | solution.py:221
  89.0 15.6 %collective-permute-start.1 = (f32[128,256]{1,0:T(8,128)S(1)}, f32[128,256]{1,0:T(8,128)S(1)}, u32[]{:S(2)}, u32[]{:S(2)}) collective-permute-start(f32[128,256]{1,0:T(8,128)S(1)} %get-tuple-element.23), channel_id=1, source_target_pairs={{0,1},{1,0},{2,9},{3,8},{4,17},{5,16},{6,25},{7,24},{8,3},{9,2},{1... | collective-permute-start | bytes 393224 | tf_op jit(solution)/shard_map/ppermute | solution.py:232
  93.6 13.3 %collective-permute-start = (f32[128,256]{1,0:T(8,128)S(1)}, f32[128,256]{1,0:T(8,128)S(1)}, u32[]{:S(2)}, u32[]{:S(2)}) collective-permute-start(f32[128,256]{1,0:T(8,128)S(1)} %get-tuple-element.24), channel_id=1, source_target_pairs={{0,0},{1,1},{2,8},{3,9},{4,16},{5,17},{6,24},{7,25},{8,2},{9,3},{1... | collective-permute-start | bytes 393224 | tf_op jit(solution)/shard_map/ppermute | solution.py:232
  96.0 1.0 copy-start.5
Sparse Core Ops, SparseCore 0:
  64.9 23.0 reduce-scatter.1

commit v3 on v2

--- a/solution.py
+++ b/solution.py
@@ -206,7 +206,6 @@
     share = block_len // dp_size
     piece = lax.dynamic_slice_in_dim(filter_taps, lax.axis_index("dp") * share, share, 0)
     piece = piece.astype(jnp.bfloat16).reshape(share, ctx_size, channels).transpose(1, 0, 2)
-    piece = lax.all_to_all(piece, "ctx", split_axis=0, concat_axis=0, tiled=True)
     packed = pl.pallas_call(
         gate_kernel,
         grid=(ctx_size // GROUP,),
@@ -215,8 +214,9 @@
         out_specs=packed_spec,
     )(queries, keys, values, cotangent)
     packed, piece = lax.optimization_barrier((packed, piece))
+    rows = lax.all_to_all(packed, "ctx", split_axis=0, concat_axis=0, tiled=True)
+    piece = lax.all_to_all(piece, "ctx", split_axis=0, concat_axis=0, tiled=True)
     taps = lax.all_gather(piece, "dp", axis=0, tiled=False)
-    rows = lax.all_to_all(packed, "ctx", split_axis=0, concat_axis=0, tiled=True)
     both, lags = local_conv(doc_lengths, rows, taps)
     back = lax.all_to_all(both, "ctx", split_axis=0, concat_axis=0, tiled=True)
     lag_share = lax.psum_scatter(lags, "dp", scatter_dimension=0, tiled=True)

time: 115 us -> 117 us (1.017)
  blocking collectives: 6.64 us -> 19.6 us
  starting transfers between devices: 19.9 us -> 14.1 us
  waiting for transfers between devices: 47.3 us -> 42.5 us
    all_to_all x0 -> x1, blocking collectives: none -> 13 us  [body(): lax.all_to_all(piece, 'ctx', split_axis=0, concat_axis=0, tiled=True)]
    all_to_all x1 -> x0, starting transfers between devices: 5.83 us -> none  [body(): lax.all_to_all(piece, 'ctx', split_axis=0, concat_axis=0, tiled=True)]
    all_to_all x1 -> x0, waiting for transfers between devices: 3.63 us -> none  [body(): lax.all_to_all(piece, 'ctx', split_axis=0, concat_axis=0, tiled=True)]
  transfers between devices with their start and end apart: 6 -> 5, of which waited for: 5 -> 4; matrix products, arithmetic and copies ran while one was open for 1% -> 1% of each run, Pallas kernels for 7% -> 3%
where the time goes in v3:
time: 117 us; the launch traced here: 116 us
  waiting for transfers between devices  42.5 us (36%)
  Pallas kernels  20.9 us (18%)
  blocking collectives  19.6 us (17%)
  between operations  14.2 us (12%)
  starting transfers between devices  14.1 us (12%)
  local copies, waits for them, and re-layouts  4.24 us (4%)
    reduce_scatter x1, waiting for transfers between devices, body(): lag_share = lax.psum_scatter(lags, 'dp', scatter_dimension=0, tiled=True)  19.1 us
    all_to_all x1, waiting for transfers between devices, body(): lax.all_to_all(packed, 'ctx', split_axis=0, concat_axis=0, tiled=True)  18 us
    pallas_call x1, Pallas kernels, local_conv(): pl.pallas_call(conv_kernel, out_shape=(jax.ShapeDtypeStruct(rows.shape, j...  13.2 us
    all_to_all x1, blocking collectives, body(): lax.all_to_all(piece, 'ctx', split_axis=0, concat_axis=0, tiled=True)  13 us
    ppermute x2, starting transfers between devices, body(): arrived.append(lax.ppermute(piece, ('dp', 'ctx'), pairs))  6.93 us
    all_gather x1, blocking collectives, body(): taps = lax.all_gather(piece, 'dp', axis=0, tiled=False)  6.64 us
    ppermute x2, waiting for transfers between devices, body(): arrived.append(lax.ppermute(piece, ('dp', 'ctx'), pairs))  5.32 us
    pallas_call x1, Pallas kernels, body(): pl.pallas_call(finish_kernel, grid=(ctx_size // GROUP,), out_shape=(jax.S...  3.98 us
  transfers between devices with their start and end apart: 5, of which 4 were waited for; matrix products, arithmetic and copies ran while one was open for 1% of the time, Pallas kernels for 3%

profile of v3, /device:TPU:2, one launch (start us, length us, event | category | flops | bytes accessed | tf_op | source)
XLA Modules:
  0.0 116.3 jit_solution(362490249336170564)
XLA Ops:
  7.2 0.0 copy-start
  7.2 1.2 %copy-done = f32[128,2048]{1,0:T(8,128)S(1)} copy-done((f32[128,2048]{1,0:T(8,128)S(1)}, f32[128,2048]{1,0:T(8,128)}, u32[]{:S(2)}) %copy-start) | copy-done | bytes 1048600
  8.4 3.7 %shard_map.119 = bf16[8,2,128,256]{3,2,1,0:T(8,128)(2,1)} custom-call(bf16[1,128,2048]{2,1,0:T(8,128)(2,1)} %query_ref.3, bf16[1,128,2048]{2,1,0:T(8,128)(2,1)} %key_ref.3, bf16[1,128,2048]{2,1,0:T(8,128)(2,1)} %value_ref.3, bf16[1,128,2048]{2,1,0:T(8,128)(2,1)} %cot_ref.3), custom_call_target="tpu_custom_call" | custom-call | tf_op jit(solution)/shard_map/pallas_call | solution.py:209
  12.2 13.0 %all_to_all.15 = bf16[8,32,256]{2,1,0:T(8,128)(2,1)S(1)} all-to-all(bf16[8,32,256]{2,1,0:T(8,128)(2,1)S(1)} %copy.15), channel_id=1, replica_groups=mesh['dp'=4,'ctx'=8] {'ctx'}, dimensions={0} | all-to-all | bytes 262144 | tf_op jit(solution)/shard_map/all_to_all | solution.py:218
  25.2 3.6 %all-to-all-start = ((bf16[8,2,128,256]{3,2,1,0:T(8,128)(2,1)}), bf16[8,2,128,256]{3,2,1,0:T(8,128)(2,1)S(1)}, u32[]{:S(2)}, u32[]{:S(2)}) async-start(bf16[8,2,128,256]{3,2,1,0:T(8,128)(2,1)} %shard_map.119), calls=%async_computation | async-start | bytes 2097152 | tf_op jit(solution)/shard_map/all_to_all | solution.py:217
  28.7 0.0 copy-start.2
  28.7 0.0 copy-start.3
  28.8 0.0 reduce-scatter.2.cloned.1.call-start
  28.8 6.6 %all-gather = bf16[32,32,256]{2,1,0:T(8,128)(2,1)S(1)} all-gather(bf16[8,32,256]{2,1,0:T(8,128)(2,1)S(1)} %all_to_all.15), channel_id=2, replica_groups=mesh['dp'=4,'ctx'=8] {'dp'}, dimensions={0}, use_global_device_ids=true | all-gather | bytes 655360 | tf_op jit(solution)/shard_map/all_gather | solution.py:219
  35.4 0.0 copy-start.4
  35.4 18.0 %all-to-all-done.rows_ref = bf16[8,2,128,256]{3,2,1,0:T(8,128)(2,1)S(1)} async-done(((bf16[8,2,128,256]{3,2,1,0:T(8,128)(2,1)}), bf16[8,2,128,256]{3,2,1,0:T(8,128)(2,1)S(1)}, u32[]{:S(2)}, u32[]{:S(2)}) %all-to-all-start) | async-done | bytes 1048608 | tf_op jit(solution)/shard_map/all_to_all | solution.py:217
  53.5 0.0 copy-done.2
  53.5 0.0 copy-done.3
  53.5 0.0 copy-done.4
  53.5 13.2 %shard_map.120 = (bf16[8,2,128,256]{3,2,1,0:T(8,128)(2,1)}, f32[1024,256]{1,0:T(8,128)S(1)}) custom-call(s32[1,4]{1,0:T(1,128)S(1)} %copy-done.4, bf16[8,2,128,256]{3,2,1,0:T(8,128)(2,1)S(1)} %all-to-all-done.rows_ref, bf16[4,8,32,256]{3,2,1,0:T(8,128)(2,1)S(1)} %bitcast.16, bf16[256,256]{1,0:T(8,128)(2,1)S(1)} %copy-done.3, bf16[128,768]{1,0:T(8,128)(2,1)S(1)} %copy-done.2), custom_call_target="tpu_custom_call" | custom-call | tf_op jit(solution)/shard_map/pallas_call | solution.py:151
  66.7 0.0 copy-start.1
  66.7 1.0 copy-done.1
  67.7 0.0 reduce-scatter.2.cloned.1.call-update
  67.7 3.6 %all-to-all-start.2 = ((bf16[8,2,128,256]{3,2,1,0:T(8,128)(2,1)}), bf16[8,2,128,256]{3,2,1,0:T(8,128)(2,1)S(1)}, u32[]{:S(2)}, u32[]{:S(2)}) async-start(bf16[8,2,128,256]{3,2,1,0:T(8,128)(2,1)} %get-tuple-element.15), calls=%async_computation.2 | async-start | bytes 2097152 | tf_op jit(solution)/shard_map/all_to_all | solution.py:221
  71.3 19.1 %reduce-scatter.2.cloned.1.call-done = f32[256,256]{1,0:T(8,128)} async-done(((f32[1024,256]{1,0:T(8,128)}), f32[256,256]{1,0:T(8,128)}) %reduce-scatter.2.cloned.1.call-update) | async-done | bytes 262160 | tf_op jit(solution)/shard_map/reduce_scatter | solution.py:222
  90.4 1.0 dynamic-slice_bitcast_fusion
  91.4 4.5 %collective-permute-start.1 = (f32[128,256]{1,0:T(8,128)S(1)}, f32[128,256]{1,0:T(8,128)S(1)}, u32[]{:S(2)}, u32[]{:S(2)}) collective-permute-start(f32[128,256]{1,0:T(8,128)S(1)} %get-tuple-element.23), channel_id=1, source_target_pairs={{0,1},{1,0},{2,9},{3,8},{4,17},{5,16},{6,25},{7,24},{8,3},{9,2},{1... | collective-permute-start | bytes 393224 | tf_op jit(solution)/shard_map/ppermute | solution.py:232
  96.0 2.4 %collective-permute-start = (f32[128,256]{1,0:T(8,128)S(1)}, f32[128,256]{1,0:T(8,128)S(1)}, u32[]{:S(2)}, u32[]{:S(2)}) collective-permute-start(f32[128,256]{1,0:T(8,128)S(1)} %get-tuple-element.24), channel_id=1, source_target_pairs={{0,0},{1,1},{2,8},{3,9},{4,16},{5,17},{6,24},{7,25},{8,2},{9,3},{1... | collective-permute-start | bytes 393224 | tf_op jit(solution)/shard_map/ppermute | solution.py:232
  98.4 0.0 all-to-all-done.2.back_ref
  98.4 0.0 copy-start.5
  98.4 1.0 copy-done.5
  99.4 4.0 %shard_map.121 = (bf16[1,128,2048]{2,1,0:T(8,128)(2,1)}, bf16[1,128,2048]{2,1,0:T(8,128)(2,1)}, bf16[1,128,2048]{2,1,0:T(8,128)(2,1)}, bf16[1,128,2048]{2,1,0:T(8,128)(2,1)}) custom-call(bf16[8,2,128,256]{3,2,1,0:T(8,128)(2,1)} %copy-done.5, bf16[1,128,2048]{2,1,0:T(8,128)(2,1)} %query_ref.3, bf16[1,128,2048]{2,1,0:T(8,128)(2,1)} %key_ref.3, ...), custom_call_target="tpu_custom_call" | custom-call | tf_op jit(solution)/shard_map/pallas_call | solution.py:241
  103.4 3.2 %collective-permute-done.1 = f32[128,256]{1,0:T(8,128)S(1)} collective-permute-done((f32[128,256]{1,0:T(8,128)S(1)}, f32[128,256]{1,0:T(8,128)S(1)}, u32[]{:S(2)}, u32[]{:S(2)}) %collective-permute-start.1) | collective-permute-done | bytes 131104 | tf_op jit(solution)/shard_map/ppermute | solution.py:232
  106.6 2.1 %collective-permute-done = f32[128,256]{1,0:T(8,128)S(1)} collective-permute-done((f32[128,256]{1,0:T(8,128)S(1)}, f32[128,256]{1,0:T(8,128)S(1)}, u32[]{:S(2)}, u32[]{:S(2)}) %collective-permute-start) | collective-permute-done | bytes 131104 | tf_op jit(solution)/shard_map/ppermute | solution.py:232
  108.7 0.1 fusion.3
  108.7 0.7 pad_maximum_fusion
  (3 shorter events, 0.1 us)
Async XLA Ops:
  7.2 1.2 %copy-start = (f32[128,2048]{1,0:T(8,128)S(1)}, f32[128,2048]{1,0:T(8,128)}, u32[]{:S(2)}) copy-start(f32[128,2048]{1,0:T(8,128)} %param.13) | copy-start | bytes 3145732
  25.2 28.3 %all-to-all-start = ((bf16[8,2,128,256]{3,2,1,0:T(8,128)(2,1)}), bf16[8,2,128,256]{3,2,1,0:T(8,128)(2,1)S(1)}, u32[]{:S(2)}, u32[]{:S(2)}) async-start(bf16[8,2,128,256]{3,2,1,0:T(8,128)(2,1)} %shard_map.119), calls=%async_computation | async-start | bytes 2097152 | tf_op jit(solution)/shard_map/all_to_all | solution.py:217
  28.7 24.7 %copy-start.2 = (bf16[128,768]{1,0:T(8,128)(2,1)S(1)}, bf16[128,768]{1,0:T(8,128)(2,1)}, u32[]{:S(2)}) copy-start(bf16[128,768]{1,0:T(8,128)(2,1)} %constant.54.clone.inv_ref) | copy-start | bytes 589828
  28.7 24.7 %copy-start.3 = (bf16[256,256]{1,0:T(8,128)(2,1)S(1)}, bf16[256,256]{1,0:T(8,128)(2,1)}, u32[]{:S(2)}) copy-start(bf16[256,256]{1,0:T(8,128)(2,1)} %constant.53.clone.fwd_ref) | copy-start | bytes 393220
  28.8 61.7 %reduce-scatter.2.cloned.1.call-start = ((), (), s32[]{:S(2)}) async-start(), calls=%async_computation.4 | async-start | bytes 1310720 | tf_op jit(solution)/shard_map/reduce_scatter | solution.py:222
  35.4 18.0 %copy-start.4 = (s32[1,4]{1,0:T(1,128)S(1)}, s32[1,4]{1,0:T(1,128)}, u32[]{:S(2)}) copy-start(s32[1,4]{1,0:T(1,128)} %lengths_ref.1) | copy-start | bytes 52
  66.7 1.0 copy-start.1
  67.7 30.7 %all-to-all-start.2 = ((bf16[8,2,128,256]{3,2,1,0:T(8,128)(2,1)}), bf16[8,2,128,256]{3,2,1,0:T(8,128)(2,1)S(1)}, u32[]{:S(2)}, u32[]{:S(2)}) async-start(bf16[8,2,128,256]{3,2,1,0:T(8,128)(2,1)} %get-tuple-element.15), calls=%async_computation.2 | async-start | bytes 2097152 | tf_op jit(solution)/shard_map/all_to_all | solution.py:221
  91.4 15.2 %collective-permute-start.1 = (f32[128,256]{1,0:T(8,128)S(1)}, f32[128,256]{1,0:T(8,128)S(1)}, u32[]{:S(2)}, u32[]{:S(2)}) collective-permute-start(f32[128,256]{1,0:T(8,128)S(1)} %get-tuple-element.23), channel_id=1, source_target_pairs={{0,1},{1,0},{2,9},{3,8},{4,17},{5,16},{6,25},{7,24},{8,3},{9,2},{1... | collective-permute-start | bytes 393224 | tf_op jit(solution)/shard_map/ppermute | solution.py:232
  96.0 12.7 %collective-permute-start = (f32[128,256]{1,0:T(8,128)S(1)}, f32[128,256]{1,0:T(8,128)S(1)}, u32[]{:S(2)}, u32[]{:S(2)}) collective-permute-start(f32[128,256]{1,0:T(8,128)S(1)} %get-tuple-element.24), channel_id=1, source_target_pairs={{0,0},{1,1},{2,8},{3,9},{4,16},{5,17},{6,24},{7,25},{8,2},{9,3},{1... | collective-permute-start | bytes 393224 | tf_op jit(solution)/shard_map/ppermute | solution.py:232
  98.4 1.0 copy-start.5
Sparse Core Ops, SparseCore 0:
  67.8 22.5 reduce-scatter.1

commit v4 on v2

--- a/solution.py
+++ b/solution.py
@@ -161,12 +161,9 @@
     )(lengths, rows, taps, jnp.asarray(fwd_table), jnp.asarray(inv_table))
 
 
-GROUP = 2
-
-
 def gate_kernel(query_ref, key_ref, value_ref, cot_ref, out_ref):
-    channels = out_ref.shape[3]
-    for part in range(GROUP):
+    blocks, _, _, channels = out_ref.shape
+    for part in range(blocks):
         cols = pl.ds(part * channels, channels)
 
         def load(ref):
@@ -179,8 +176,8 @@
 def finish_kernel(
     back_ref, query_ref, key_ref, value_ref, cot_ref, out_ref, dquery_ref, dkey_ref, dvalue_ref
 ):
-    channels = back_ref.shape[3]
-    for part in range(GROUP):
+    blocks, _, _, channels = back_ref.shape
+    for part in range(blocks):
         cols = pl.ds(part * channels, channels)
 
         def load(ref):
@@ -201,18 +198,18 @@
     ratio = ctx_size // dp_size
     ctx_rank = lax.axis_index("ctx")
     channels = width // ctx_size
-    wide = pl.BlockSpec((1, block_len, GROUP * channels), lambda i: (0, 0, i))
-    packed_spec = pl.BlockSpec((GROUP, 2, block_len, channels), lambda i: (i, 0, 0, 0))
+    vmem = pl.BlockSpec(memory_space=pltpu.VMEM)
+    params = pltpu.CompilerParams(vmem_limit_bytes=16 * 1024 * 1024)
     share = block_len // dp_size
     piece = lax.dynamic_slice_in_dim(filter_taps, lax.axis_index("dp") * share, share, 0)
     piece = piece.astype(jnp.bfloat16).reshape(share, ctx_size, channels).transpose(1, 0, 2)
     piece = lax.all_to_all(piece, "ctx", split_axis=0, concat_axis=0, tiled=True)
     packed = pl.pallas_call(
         gate_kernel,
-        grid=(ctx_size // GROUP,),
         out_shape=jax.ShapeDtypeStruct((ctx_size, 2, block_len, channels), jnp.bfloat16),
-        in_specs=[wide] * 4,
-        out_specs=packed_spec,
+        in_specs=[vmem] * 4,
+        out_specs=vmem,
+        compiler_params=params,
     )(queries, keys, values, cotangent)
     packed, piece = lax.optimization_barrier((packed, piece))
     taps = lax.all_gather(piece, "dp", axis=0, tiled=False)
@@ -240,10 +237,10 @@
     )
     outs = pl.pallas_call(
         finish_kernel,
-        grid=(ctx_size // GROUP,),
         out_shape=(jax.ShapeDtypeStruct(queries.shape, jnp.bfloat16),) * 4,
-        in_specs=[packed_spec] + [wide] * 4,
-        out_specs=(wide,) * 4,
+        in_specs=[vmem] * 5,
+        out_specs=(vmem,) * 4,
+        compiler_params=params,
     )(back, queries, keys, values, cotangent)
     return (*outs, grad_filter)
 

time: 115 us -> 116 us (level)
  Pallas kernels: 20.8 us -> 15 us
  local copies, waits for them, and re-layouts: 4.91 us -> 10.4 us
    pallas_call x2, Pallas kernels: 7.69 us -> 2.82 us  [the longest x1 1.56 us: body(): pl.pallas_call(finish_kernel, out_shape=(jax.ShapeDtypeStruct(queries.sha...]
    unnamed x13 -> x29, local copies, waits for them, and re-layouts: 3.23 us -> 8.06 us
  transfers between devices with their start and end apart: 6 -> 6, of which waited for: 5 -> 5; matrix products, arithmetic and copies ran while one was open for 1% -> 1% of each run, Pallas kernels for 7% -> 2%
where the time goes in v4:
time: 116 us; the launch traced here: 115 us
  waiting for transfers between devices  48.1 us (41%)
  starting transfers between devices  19.9 us (17%)
  Pallas kernels  15 us (13%)
  between operations  14.2 us (12%)
  local copies, waits for them, and re-layouts  10.4 us (9%)
  blocking collectives  6.85 us (6%)
    reduce_scatter x1, waiting for transfers between devices, body(): lag_share = lax.psum_scatter(lags, 'dp', scatter_dimension=0, tiled=True)  19.5 us
    all_to_all x1, waiting for transfers between devices, body(): lax.all_to_all(packed, 'ctx', split_axis=0, concat_axis=0, tiled=True)  17.8 us
    pallas_call x1, Pallas kernels, local_conv(): pl.pallas_call(conv_kernel, out_shape=(jax.ShapeDtypeStruct(rows.shape, j...  12.1 us
    unnamed x29, local copies, waits for them, and re-layouts  8.06 us
    ppermute x2, starting transfers between devices, body(): arrived.append(lax.ppermute(piece, ('dp', 'ctx'), pairs))  6.86 us
    all_gather x1, blocking collectives, body(): taps = lax.all_gather(piece, 'dp', axis=0, tiled=False)  6.85 us
    ppermute x2, waiting for transfers between devices, body(): arrived.append(lax.ppermute(piece, ('dp', 'ctx'), pairs))  6.82 us
    all_to_all x1, starting transfers between devices, body(): lax.all_to_all(piece, 'ctx', split_axis=0, concat_axis=0, tiled=True)  5.83 us
  transfers between devices with their start and end apart: 6, of which 5 were waited for; matrix products, arithmetic and copies ran while one was open for 1% of the time, Pallas kernels for 2%

profile of v4, /device:TPU:2, one launch (start us, length us, event | category | flops | bytes accessed | tf_op | source)
XLA Modules:
  0.0 115.2 jit_solution(5746656146984770916)
XLA Ops:
  7.2 0.0 copy-start
  7.2 1.2 %copy-done = f32[128,2048]{1,0:T(8,128)S(1)} copy-done((f32[128,2048]{1,0:T(8,128)S(1)}, f32[128,2048]{1,0:T(8,128)}, u32[]{:S(2)}) %copy-start) | copy-done | bytes 1048600
  8.4 0.0 copy-start.1
  8.4 0.0 copy-start.2
  8.5 0.7 copy.15
  9.1 5.8 %all-to-all-start = ((bf16[8,32,256]{2,1,0:T(8,128)(2,1)}), bf16[8,32,256]{2,1,0:T(8,128)(2,1)S(1)}, u32[]{:S(2)}, u32[]{:S(2)}) async-start(bf16[8,32,256]{2,1,0:T(8,128)(2,1)} %copy.15), calls=%async_computation | async-start | bytes 262144 | tf_op jit(solution)/shard_map/all_to_all | solution.py:206
  15.0 0.0 copy-done.1
  15.0 0.0 copy-done.2
  15.0 0.0 copy-start.4
  15.0 1.0 copy-done.4
  16.0 0.0 copy-start.6
  16.0 1.0 copy-done.6
  17.1 1.3 %shard_map.119 = bf16[8,2,128,256]{3,2,1,0:T(8,128)(2,1)} custom-call(bf16[1,128,2048]{2,1,0:T(8,128)(2,1)S(1)} %copy-done.1, bf16[1,128,2048]{2,1,0:T(8,128)(2,1)S(1)} %copy-done.2, bf16[1,128,2048]{2,1,0:T(8,128)(2,1)S(1)} %copy-done.4, bf16[1,128,2048]{2,1,0:T(8,128)(2,1)S(1)} %copy-done.6), custom_call_target="tpu_custom_call" | custom-call | tf_op jit(solution)/shard_map/pallas_call | solution.py:207
  18.3 4.0 %all-to-all-done = bf16[8,32,256]{2,1,0:T(8,128)(2,1)S(1)} async-done(((bf16[8,32,256]{2,1,0:T(8,128)(2,1)}), bf16[8,32,256]{2,1,0:T(8,128)(2,1)S(1)}, u32[]{:S(2)}, u32[]{:S(2)}) %all-to-all-start) | async-done | bytes 131104 | tf_op jit(solution)/shard_map/all_to_all | solution.py:206
  22.3 0.0 copy-start.13
  22.3 0.7 copy-done.13
  23.0 3.6 %all-to-all-start.1 = ((bf16[8,2,128,256]{3,2,1,0:T(8,128)(2,1)}), bf16[8,2,128,256]{3,2,1,0:T(8,128)(2,1)S(1)}, u32[]{:S(2)}, u32[]{:S(2)}) async-start(bf16[8,2,128,256]{3,2,1,0:T(8,128)(2,1)} %shard_map.119), calls=%async_computation.1 | async-start | bytes 2097152 | tf_op jit(solution)/shard_map/all_to_all | solution.py:216
  26.5 0.0 copy-start.10
  26.5 0.0 copy-start.11
  26.6 0.0 reduce-scatter.2.cloned.1.call-start
  26.6 6.9 %all-gather = bf16[32,32,256]{2,1,0:T(8,128)(2,1)S(1)} all-gather(bf16[8,32,256]{2,1,0:T(8,128)(2,1)} %copy-done.13), channel_id=2, replica_groups=mesh['dp'=4,'ctx'=8] {'dp'}, dimensions={0}, use_global_device_ids=true | all-gather | bytes 655360 | tf_op jit(solution)/shard_map/all_gather | solution.py:215
  33.5 0.0 copy-start.12
  33.5 17.8 %all-to-all-done.1.rows_ref = bf16[8,2,128,256]{3,2,1,0:T(8,128)(2,1)S(1)} async-done(((bf16[8,2,128,256]{3,2,1,0:T(8,128)(2,1)}), bf16[8,2,128,256]{3,2,1,0:T(8,128)(2,1)S(1)}, u32[]{:S(2)}, u32[]{:S(2)}) %all-to-all-start.1) | async-done | bytes 1048608 | tf_op jit(solution)/shard_map/all_to_all | solution.py:216
  51.3 0.0 copy-done.10
  51.3 0.0 copy-done.11
  51.3 0.0 copy-done.12
  51.3 12.1 %shard_map.120 = (bf16[8,2,128,256]{3,2,1,0:T(8,128)(2,1)S(1)}, f32[1024,256]{1,0:T(8,128)S(1)}) custom-call(s32[1,4]{1,0:T(1,128)S(1)} %copy-done.12, bf16[8,2,128,256]{3,2,1,0:T(8,128)(2,1)S(1)} %all-to-all-done.1.rows_ref, bf16[4,8,32,256]{3,2,1,0:T(8,128)(2,1)S(1)} %bitcast.16, bf16[256,256]{1,0:T(8,128)(2,1)S(1)} %copy-done.11, ...), custom_call_target="tpu_custom_call" | custom-call | tf_op jit(solution)/shard_map/pallas_call | solution.py:151
  63.4 0.0 copy-start.8
  63.5 1.0 copy-done.8
  64.5 0.0 copy-start.9
  64.5 1.0 copy-done.9
  65.4 0.0 reduce-scatter.2.cloned.1.call-update
  65.4 3.6 %all-to-all-start.2 = ((bf16[8,2,128,256]{3,2,1,0:T(8,128)(2,1)}), bf16[8,2,128,256]{3,2,1,0:T(8,128)(2,1)S(1)}, u32[]{:S(2)}, u32[]{:S(2)}) async-start(bf16[8,2,128,256]{3,2,1,0:T(8,128)(2,1)} %copy-done.8), calls=%async_computation.2 | async-start | bytes 2097152 | tf_op jit(solution)/shard_map/all_to_all | solution.py:218
  69.0 0.0 copy-start.3
  69.1 19.5 %reduce-scatter.2.cloned.1.call-done = f32[256,256]{1,0:T(8,128)} async-done(((f32[1024,256]{1,0:T(8,128)}), f32[256,256]{1,0:T(8,128)}) %reduce-scatter.2.cloned.1.call-update) | async-done | bytes 262160 | tf_op jit(solution)/shard_map/reduce_scatter | solution.py:219
  88.6 1.6 %dynamic-slice_bitcast_fusion = (f32[128,256]{1,0:T(8,128)}, f32[128,256]{1,0:T(8,128)S(1)}) fusion(f32[2,128,256]{2,1,0:T(8,128)} %bitcast.19, s32[]{:T(128)S(6)} %select_n.35, s32[]{:T(128)S(6)} %select_n.33), kind=kLoop, calls=%fused_computation.10 | loop fusion | bytes 524296 | tf_op jit(solution)/shard_map/jit(dynamic_index_in_dim)/squeeze | solution.py:228
  90.2 4.4 %collective-permute-start.1 = (f32[128,256]{1,0:T(8,128)}, f32[128,256]{1,0:T(8,128)S(1)}, u32[]{:S(2)}, u32[]{:S(2)}) collective-permute-start(f32[128,256]{1,0:T(8,128)} %get-tuple-element.23), channel_id=1, source_target_pairs={{0,1},{1,0},{2,9},{3,8},{4,17},{5,16},{6,25},{7,24},{8,3},{9,2},{1... | collective-permute-start | bytes 393224 | tf_op jit(solution)/shard_map/ppermute | solution.py:229
  94.6 2.4 %collective-permute-start = (f32[128,256]{1,0:T(8,128)S(1)}, f32[128,256]{1,0:T(8,128)S(1)}, u32[]{:S(2)}, u32[]{:S(2)}) collective-permute-start(f32[128,256]{1,0:T(8,128)S(1)} %get-tuple-element.24), channel_id=1, source_target_pairs={{0,0},{1,1},{2,8},{3,9},{4,16},{5,17},{6,24},{7,25},{8,2},{9,3},{1... | collective-permute-start | bytes 393224 | tf_op jit(solution)/shard_map/ppermute | solution.py:229
  97.1 0.0 all-to-all-done.2.back_ref
  97.1 0.0 copy-done.3
  97.1 0.0 copy-start.5
  97.1 1.0 copy-done.5
  98.2 0.0 copy-start.7
  98.2 1.0 copy-done.7
  99.2 1.6 %shard_map.121 = (bf16[1,128,2048]{2,1,0:T(8,128)(2,1)}, bf16[1,128,2048]{2,1,0:T(8,128)(2,1)}, bf16[1,128,2048]{2,1,0:T(8,128)(2,1)}, bf16[1,128,2048]{2,1,0:T(8,128)(2,1)}) custom-call(bf16[8,2,128,256]{3,2,1,0:T(8,128)(2,1)S(1)} %all-to-all-done.2.back_ref, bf16[1,128,2048]{2,1,0:T(8,128)(2,1)S(1)} %copy-done.1, bf16[1,128,2048]{2,1,0:T(8,128)(2,1)S(1)} %copy-done.3, ...), custom_call_target="tpu_custom_call" | custom-call | tf_op jit(solution)/shard_map/pallas_call | solution.py:238
  100.8 4.3 %collective-permute-done.1 = f32[128,256]{1,0:T(8,128)S(1)} collective-permute-done((f32[128,256]{1,0:T(8,128)}, f32[128,256]{1,0:T(8,128)S(1)}, u32[]{:S(2)}, u32[]{:S(2)}) %collective-permute-start.1) | collective-permute-done | bytes 131104 | tf_op jit(solution)/shard_map/ppermute | solution.py:229
  105.1 2.5 %collective-permute-done = f32[128,256]{1,0:T(8,128)S(1)} collective-permute-done((f32[128,256]{1,0:T(8,128)S(1)}, f32[128,256]{1,0:T(8,128)S(1)}, u32[]{:S(2)}, u32[]{:S(2)}) %collective-permute-start) | collective-permute-done | bytes 131104 | tf_op jit(solution)/shard_map/ppermute | solution.py:229
  107.6 0.1 fusion.3
  107.7 0.7 pad_maximum_fusion
  (2 shorter events, 0.0 us)
Async XLA Ops:
  7.2 1.2 %copy-start = (f32[128,2048]{1,0:T(8,128)S(1)}, f32[128,2048]{1,0:T(8,128)}, u32[]{:S(2)}) copy-start(f32[128,2048]{1,0:T(8,128)} %param.13) | copy-start | bytes 3145732
  8.4 6.6 %copy-start.1 = (bf16[1,128,2048]{2,1,0:T(8,128)(2,1)S(1)}, bf16[1,128,2048]{2,1,0:T(8,128)(2,1)}, u32[]{:S(2)}) copy-start(bf16[1,128,2048]{2,1,0:T(8,128)(2,1)} %query_ref.3) | copy-start | bytes 1572868
  8.4 6.6 %copy-start.2 = (bf16[1,128,2048]{2,1,0:T(8,128)(2,1)S(1)}, bf16[1,128,2048]{2,1,0:T(8,128)(2,1)}, u32[]{:S(2)}) copy-start(bf16[1,128,2048]{2,1,0:T(8,128)(2,1)} %key_ref.3) | copy-start | bytes 1572868
  9.1 13.2 %all-to-all-start = ((bf16[8,32,256]{2,1,0:T(8,128)(2,1)}), bf16[8,32,256]{2,1,0:T(8,128)(2,1)S(1)}, u32[]{:S(2)}, u32[]{:S(2)}) async-start(bf16[8,32,256]{2,1,0:T(8,128)(2,1)} %copy.15), calls=%async_computation | async-start | bytes 262144 | tf_op jit(solution)/shard_map/all_to_all | solution.py:206
  15.0 1.0 copy-start.4
  16.0 1.0 copy-start.6
  22.3 0.7 copy-start.13
  23.0 28.3 %all-to-all-start.1 = ((bf16[8,2,128,256]{3,2,1,0:T(8,128)(2,1)}), bf16[8,2,128,256]{3,2,1,0:T(8,128)(2,1)S(1)}, u32[]{:S(2)}, u32[]{:S(2)}) async-start(bf16[8,2,128,256]{3,2,1,0:T(8,128)(2,1)} %shard_map.119), calls=%async_computation.1 | async-start | bytes 2097152 | tf_op jit(solution)/shard_map/all_to_all | solution.py:216
  26.5 24.7 %copy-start.10 = (bf16[128,768]{1,0:T(8,128)(2,1)S(1)}, bf16[128,768]{1,0:T(8,128)(2,1)}, u32[]{:S(2)}) copy-start(bf16[128,768]{1,0:T(8,128)(2,1)} %constant.54.clone.inv_ref) | copy-start | bytes 589828
  26.5 24.7 %copy-start.11 = (bf16[256,256]{1,0:T(8,128)(2,1)S(1)}, bf16[256,256]{1,0:T(8,128)(2,1)}, u32[]{:S(2)}) copy-start(bf16[256,256]{1,0:T(8,128)(2,1)} %constant.53.clone.fwd_ref) | copy-start | bytes 393220
  26.6 62.0 %reduce-scatter.2.cloned.1.call-start = ((), (), s32[]{:S(2)}) async-start(), calls=%async_computation.4 | async-start | bytes 1310720 | tf_op jit(solution)/shard_map/reduce_scatter | solution.py:219
  33.5 17.8 %copy-start.12 = (s32[1,4]{1,0:T(1,128)S(1)}, s32[1,4]{1,0:T(1,128)}, u32[]{:S(2)}) copy-start(s32[1,4]{1,0:T(1,128)} %lengths_ref.1) | copy-start | bytes 52
  63.4 1.0 copy-start.8
  64.5 1.0 copy-start.9
  65.4 31.7 %all-to-all-start.2 = ((bf16[8,2,128,256]{3,2,1,0:T(8,128)(2,1)}), bf16[8,2,128,256]{3,2,1,0:T(8,128)(2,1)S(1)}, u32[]{:S(2)}, u32[]{:S(2)}) async-start(bf16[8,2,128,256]{3,2,1,0:T(8,128)(2,1)} %copy-done.8), calls=%async_computation.2 | async-start | bytes 2097152 | tf_op jit(solution)/shard_map/all_to_all | solution.py:218
  69.0 28.1 %copy-start.3 = (bf16[1,128,2048]{2,1,0:T(8,128)(2,1)S(1)}, bf16[1,128,2048]{2,1,0:T(8,128)(2,1)}, u32[]{:S(2)}) copy-start(bf16[1,128,2048]{2,1,0:T(8,128)(2,1)} %key_ref.3) | copy-start | bytes 1572868
  90.2 14.9 %collective-permute-start.1 = (f32[128,256]{1,0:T(8,128)}, f32[128,256]{1,0:T(8,128)S(1)}, u32[]{:S(2)}, u32[]{:S(2)}) collective-permute-start(f32[128,256]{1,0:T(8,128)} %get-tuple-element.23), channel_id=1, source_target_pairs={{0,1},{1,0},{2,9},{3,8},{4,17},{5,16},{6,25},{7,24},{8,3},{9,2},{1... | collective-permute-start | bytes 393224 | tf_op jit(solution)/shard_map/ppermute | solution.py:229
  94.6 13.0 %collective-permute-start = (f32[128,256]{1,0:T(8,128)S(1)}, f32[128,256]{1,0:T(8,128)S(1)}, u32[]{:S(2)}, u32[]{:S(2)}) collective-permute-start(f32[128,256]{1,0:T(8,128)S(1)} %get-tuple-element.24), channel_id=1, source_target_pairs={{0,0},{1,1},{2,8},{3,9},{4,16},{5,17},{6,24},{7,25},{8,2},{9,3},{1... | collective-permute-start | bytes 393224 | tf_op jit(solution)/shard_map/ppermute | solution.py:229
  97.1 1.0 copy-start.5
  98.2 1.0 copy-start.7
Sparse Core Ops, SparseCore 0:
  65.6 22.9 reduce-scatter.1

commit v5 on v2

--- a/solution.py
+++ b/solution.py
@@ -137,9 +137,10 @@
     def _(block):
         real = lag_spec[block, :block_len] + sign * lag_spec[block + 1, block_len:]
         imag = lag_spec[block, block_len:] - sign * lag_spec[block + 1, :block_len]
-        lag_ref[rows_at(block), :] = inverse(jnp.concatenate([real, imag], axis=0))
-
-    lag_ref[rows_at(blocks - 1), :] = inverse(lag_spec[blocks - 1])
+        total = inverse(jnp.concatenate([real, imag], axis=0))
+        lag_ref[rows_at(block), :] = total.astype(jnp.bfloat16)
+
+    lag_ref[rows_at(blocks - 1), :] = inverse(lag_spec[blocks - 1]).astype(jnp.bfloat16)
 
 
 def local_conv(lengths, rows, taps):
@@ -152,7 +153,7 @@
         conv_kernel,
         out_shape=(
             jax.ShapeDtypeStruct(rows.shape, jnp.bfloat16),
-            jax.ShapeDtypeStruct((seq, channels), jnp.float32),
+            jax.ShapeDtypeStruct((seq, channels), jnp.bfloat16),
         ),
         in_specs=[pl.BlockSpec(memory_space=pltpu.SMEM), vmem, vmem, vmem, vmem],
         out_specs=(vmem, vmem),
@@ -237,7 +238,7 @@
             for m in range(ratio)
         ],
         axis=1,
-    )
+    ).astype(jnp.float32)
     outs = pl.pallas_call(
         finish_kernel,
         grid=(ctx_size // GROUP,),

time: 115 us -> 123 us (1.070); the launches traced: 115 us -> 121 us
  waiting for transfers between devices: 47.3 us -> 53.1 us
    reduce_scatter x1, waiting for transfers between devices: 19.7 us -> 25 us  [body(): lag_share = lax.psum_scatter(lags, 'dp', scatter_dimension=0, tiled=True)]
  transfers between devices with their start and end apart: 6 -> 6, of which waited for: 5 -> 5; matrix products, arithmetic and copies ran while one was open for 1% -> 1% of each run, Pallas kernels for 7% -> 3%
where the time goes in v5:
time: 123 us; the launch traced here: 121 us
  waiting for transfers between devices  53.1 us (43%)
  Pallas kernels  21.3 us (17%)
  starting transfers between devices  19.9 us (16%)
  between operations  14.2 us (12%)
  blocking collectives  6.64 us (5%)
  local copies, waits for them, and re-layouts  4.8 us (4%)
    reduce_scatter x1, waiting for transfers between devices, body(): lag_share = lax.psum_scatter(lags, 'dp', scatter_dimension=0, tiled=True)  25 us
    all_to_all x1, waiting for transfers between devices, body(): lax.all_to_all(packed, 'ctx', split_axis=0, concat_axis=0, tiled=True)  18.1 us
    pallas_call x1, Pallas kernels, local_conv(): pl.pallas_call(conv_kernel, out_shape=(jax.ShapeDtypeStruct(rows.shape, j...  13.6 us
    ppermute x2, starting transfers between devices, body(): arrived.append(lax.ppermute(piece, ('dp', 'ctx'), pairs))  6.93 us
    all_gather x1, blocking collectives, body(): taps = lax.all_gather(piece, 'dp', axis=0, tiled=False)  6.64 us
    all_to_all x1, starting transfers between devices, body(): lax.all_to_all(piece, 'ctx', split_axis=0, concat_axis=0, tiled=True)  5.83 us
    ppermute x2, waiting for transfers between devices, body(): arrived.append(lax.ppermute(piece, ('dp', 'ctx'), pairs))  5.72 us
    pallas_call x1, Pallas kernels, body(): pl.pallas_call(finish_kernel, grid=(ctx_size // GROUP,), out_shape=(jax.S...  3.98 us
  transfers between devices with their start and end apart: 6, of which 5 were waited for; matrix products, arithmetic and copies ran while one was open for 1% of the time, Pallas kernels for 3%

profile of v5, /device:TPU:2, one launch (start us, length us, event | category | flops | bytes accessed | tf_op | source)
XLA Modules:
  0.0 120.7 jit_solution(11555301830110131683)
XLA Ops:
  7.2 0.0 copy-start
  7.2 1.2 %copy-done = f32[128,2048]{1,0:T(8,128)S(1)} copy-done((f32[128,2048]{1,0:T(8,128)S(1)}, f32[128,2048]{1,0:T(8,128)}, u32[]{:S(2)}) %copy-start) | copy-done | bytes 1048600
  8.4 0.7 copy.15
  9.1 5.8 %all-to-all-start = ((bf16[8,32,256]{2,1,0:T(8,128)(2,1)}), bf16[8,32,256]{2,1,0:T(8,128)(2,1)S(1)}, u32[]{:S(2)}, u32[]{:S(2)}) async-start(bf16[8,32,256]{2,1,0:T(8,128)(2,1)} %copy.15), calls=%async_computation | async-start | bytes 262144 | tf_op jit(solution)/shard_map/all_to_all | solution.py:210
  15.0 3.7 %shard_map.119 = bf16[8,2,128,256]{3,2,1,0:T(8,128)(2,1)} custom-call(bf16[1,128,2048]{2,1,0:T(8,128)(2,1)} %query_ref.3, bf16[1,128,2048]{2,1,0:T(8,128)(2,1)} %key_ref.3, bf16[1,128,2048]{2,1,0:T(8,128)(2,1)} %value_ref.3, bf16[1,128,2048]{2,1,0:T(8,128)(2,1)} %cot_ref.3), custom_call_target="tpu_custom_call" | custom-call | tf_op jit(solution)/shard_map/pallas_call | solution.py:211
  18.7 3.6 %all-to-all-done = bf16[8,32,256]{2,1,0:T(8,128)(2,1)S(1)} async-done(((bf16[8,32,256]{2,1,0:T(8,128)(2,1)}), bf16[8,32,256]{2,1,0:T(8,128)(2,1)S(1)}, u32[]{:S(2)}, u32[]{:S(2)}) %all-to-all-start) | async-done | bytes 131104 | tf_op jit(solution)/shard_map/all_to_all | solution.py:210
  22.3 3.6 %all-to-all-start.1 = ((bf16[8,2,128,256]{3,2,1,0:T(8,128)(2,1)}), bf16[8,2,128,256]{3,2,1,0:T(8,128)(2,1)S(1)}, u32[]{:S(2)}, u32[]{:S(2)}) async-start(bf16[8,2,128,256]{3,2,1,0:T(8,128)(2,1)} %shard_map.119), calls=%async_computation.1 | async-start | bytes 2097152 | tf_op jit(solution)/shard_map/all_to_all | solution.py:220
  25.9 0.0 copy-start.2
  25.9 0.0 copy-start.3
  25.9 6.6 %all-gather = bf16[32,32,256]{2,1,0:T(8,128)(2,1)S(1)} all-gather(bf16[8,32,256]{2,1,0:T(8,128)(2,1)S(1)} %all-to-all-done), channel_id=2, replica_groups=mesh['dp'=4,'ctx'=8] {'dp'}, dimensions={0}, use_global_device_ids=true | all-gather | bytes 655360 | tf_op jit(solution)/shard_map/all_gather | solution.py:219
  32.5 0.0 copy-start.4
  32.5 18.1 %all-to-all-done.1.rows_ref = bf16[8,2,128,256]{3,2,1,0:T(8,128)(2,1)S(1)} async-done(((bf16[8,2,128,256]{3,2,1,0:T(8,128)(2,1)}), bf16[8,2,128,256]{3,2,1,0:T(8,128)(2,1)S(1)}, u32[]{:S(2)}, u32[]{:S(2)}) %all-to-all-start.1) | async-done | bytes 1048608 | tf_op jit(solution)/shard_map/all_to_all | solution.py:220
  50.6 0.0 copy-done.2
  50.6 0.0 copy-done.3
  50.6 0.0 copy-done.4
  50.6 13.6 %shard_map.120 = (bf16[8,2,128,256]{3,2,1,0:T(8,128)(2,1)S(1)}, bf16[1024,256]{1,0:T(8,128)(2,1)}) custom-call(s32[1,4]{1,0:T(1,128)S(1)} %copy-done.4, bf16[8,2,128,256]{3,2,1,0:T(8,128)(2,1)S(1)} %all-to-all-done.1.rows_ref, bf16[4,8,32,256]{3,2,1,0:T(8,128)(2,1)S(1)} %bitcast.16, bf16[256,256]{1,0:T(8,128)(2,1)S(1)} %copy-done.3, ...), custom_call_target="tpu_custom_call" | custom-call | tf_op jit(solution)/shard_map/pallas_call | solution.py:152
  64.2 0.0 copy-start.1
  64.2 1.0 copy-done.1
  65.2 3.6 %all-to-all-start.2 = ((bf16[8,2,128,256]{3,2,1,0:T(8,128)(2,1)}), bf16[8,2,128,256]{3,2,1,0:T(8,128)(2,1)S(1)}, u32[]{:S(2)}, u32[]{:S(2)}) async-start(bf16[8,2,128,256]{3,2,1,0:T(8,128)(2,1)} %copy-done.1), calls=%async_computation.2 | async-start | bytes 2097152 | tf_op jit(solution)/shard_map/all_to_all | solution.py:222
  68.8 0.0 reduce-scatter.2.cloned.1.call-start
  68.8 0.7 reduce-scatter.2.cloned.1.call-update
  69.6 25.0 %reduce-scatter.2.cloned.1.call-done = bf16[256,256]{1,0:T(8,128)(2,1)} async-done(((bf16[1024,256]{1,0:T(8,128)(2,1)}), bf16[256,256]{1,0:T(8,128)(2,1)}) %reduce-scatter.2.cloned.1.call-update) | async-done | bytes 131088 | tf_op jit(solution)/shard_map/reduce_scatter | solution.py:223
  94.5 0.9 dynamic-slice_bitcast_fusion
  95.4 4.5 %collective-permute-start.1 = (bf16[128,256]{1,0:T(8,128)(2,1)S(1)}, bf16[128,256]{1,0:T(8,128)(2,1)S(1)}, u32[]{:S(2)}, u32[]{:S(2)}) collective-permute-start(bf16[128,256]{1,0:T(8,128)(2,1)S(1)} %get-tuple-element.23), channel_id=1, source_target_pairs={{0,1},{1,0},{2,9},{3,8},{4,17},{5,16},{6,25},{7,24},{8,3},{9,2},{1... | collective-permute-start | bytes 196616 | tf_op jit(solution)/shard_map/ppermute | solution.py:233
  99.9 2.4 %collective-permute-start = (bf16[128,256]{1,0:T(8,128)(2,1)S(1)}, bf16[128,256]{1,0:T(8,128)(2,1)S(1)}, u32[]{:S(2)}, u32[]{:S(2)}) collective-permute-start(bf16[128,256]{1,0:T(8,128)(2,1)S(1)} %get-tuple-element.24), channel_id=1, source_target_pairs={{0,0},{1,1},{2,8},{3,9},{4,16},{5,17},{6,24},{7,25},{8,2},{9,3},{1... | collective-permute-start | bytes 196616 | tf_op jit(solution)/shard_map/ppermute | solution.py:233
  102.4 1.9 %collective-permute-done.1 = bf16[128,256]{1,0:T(8,128)(2,1)S(1)} collective-permute-done((bf16[128,256]{1,0:T(8,128)(2,1)S(1)}, bf16[128,256]{1,0:T(8,128)(2,1)S(1)}, u32[]{:S(2)}, u32[]{:S(2)}) %collective-permute-start.1) | collective-permute-done | bytes 65568 | tf_op jit(solution)/shard_map/ppermute | solution.py:233
  104.2 3.9 %collective-permute-done = bf16[128,256]{1,0:T(8,128)(2,1)S(1)} collective-permute-done((bf16[128,256]{1,0:T(8,128)(2,1)S(1)}, bf16[128,256]{1,0:T(8,128)(2,1)S(1)}, u32[]{:S(2)}, u32[]{:S(2)}) %collective-permute-start) | collective-permute-done | bytes 65568 | tf_op jit(solution)/shard_map/ppermute | solution.py:233
  108.1 0.1 fusion.3
  108.2 0.7 maximum_convert_fusion
  108.9 0.0 all-to-all-done.2.back_ref
  108.9 0.0 copy-start.5
  108.9 1.0 copy-done.5
  109.9 4.0 %shard_map.121 = (bf16[1,128,2048]{2,1,0:T(8,128)(2,1)}, bf16[1,128,2048]{2,1,0:T(8,128)(2,1)}, bf16[1,128,2048]{2,1,0:T(8,128)(2,1)}, bf16[1,128,2048]{2,1,0:T(8,128)(2,1)}) custom-call(bf16[8,2,128,256]{3,2,1,0:T(8,128)(2,1)} %copy-done.5, bf16[1,128,2048]{2,1,0:T(8,128)(2,1)} %query_ref.3, bf16[1,128,2048]{2,1,0:T(8,128)(2,1)} %key_ref.3, ...), custom_call_target="tpu_custom_call" | custom-call | tf_op jit(solution)/shard_map/pallas_call | solution.py:242
  (2 shorter events, 0.0 us)
Async XLA Ops:
  7.2 1.2 %copy-start = (f32[128,2048]{1,0:T(8,128)S(1)}, f32[128,2048]{1,0:T(8,128)}, u32[]{:S(2)}) copy-start(f32[128,2048]{1,0:T(8,128)} %param.13) | copy-start | bytes 3145732
  9.1 13.2 %all-to-all-start = ((bf16[8,32,256]{2,1,0:T(8,128)(2,1)}), bf16[8,32,256]{2,1,0:T(8,128)(2,1)S(1)}, u32[]{:S(2)}, u32[]{:S(2)}) async-start(bf16[8,32,256]{2,1,0:T(8,128)(2,1)} %copy.15), calls=%async_computation | async-start | bytes 262144 | tf_op jit(solution)/shard_map/all_to_all | solution.py:210
  22.3 28.3 %all-to-all-start.1 = ((bf16[8,2,128,256]{3,2,1,0:T(8,128)(2,1)}), bf16[8,2,128,256]{3,2,1,0:T(8,128)(2,1)S(1)}, u32[]{:S(2)}, u32[]{:S(2)}) async-start(bf16[8,2,128,256]{3,2,1,0:T(8,128)(2,1)} %shard_map.119), calls=%async_computation.1 | async-start | bytes 2097152 | tf_op jit(solution)/shard_map/all_to_all | solution.py:220
  25.9 24.7 %copy-start.2 = (bf16[128,768]{1,0:T(8,128)(2,1)S(1)}, bf16[128,768]{1,0:T(8,128)(2,1)}, u32[]{:S(2)}) copy-start(bf16[128,768]{1,0:T(8,128)(2,1)} %constant.54.clone.inv_ref) | copy-start | bytes 589828
  25.9 24.7 %copy-start.3 = (bf16[256,256]{1,0:T(8,128)(2,1)S(1)}, bf16[256,256]{1,0:T(8,128)(2,1)}, u32[]{:S(2)}) copy-start(bf16[256,256]{1,0:T(8,128)(2,1)} %constant.53.clone.fwd_ref) | copy-start | bytes 393220
  32.5 18.1 %copy-start.4 = (s32[1,4]{1,0:T(1,128)S(1)}, s32[1,4]{1,0:T(1,128)}, u32[]{:S(2)}) copy-start(s32[1,4]{1,0:T(1,128)} %lengths_ref.1) | copy-start | bytes 52
  64.2 1.0 copy-start.1
  65.2 43.7 %all-to-all-start.2 = ((bf16[8,2,128,256]{3,2,1,0:T(8,128)(2,1)}), bf16[8,2,128,256]{3,2,1,0:T(8,128)(2,1)S(1)}, u32[]{:S(2)}, u32[]{:S(2)}) async-start(bf16[8,2,128,256]{3,2,1,0:T(8,128)(2,1)} %copy-done.1), calls=%async_computation.2 | async-start | bytes 2097152 | tf_op jit(solution)/shard_map/all_to_all | solution.py:222
  68.8 25.7 %reduce-scatter.2.cloned.1.call-start = ((), (), s32[]{:S(2)}) async-start(), calls=%async_computation.4 | async-start | bytes 655360 | tf_op jit(solution)/shard_map/reduce_scatter | solution.py:223
  95.4 8.8 %collective-permute-start.1 = (bf16[128,256]{1,0:T(8,128)(2,1)S(1)}, bf16[128,256]{1,0:T(8,128)(2,1)S(1)}, u32[]{:S(2)}, u32[]{:S(2)}) collective-permute-start(bf16[128,256]{1,0:T(8,128)(2,1)S(1)} %get-tuple-element.23), channel_id=1, source_target_pairs={{0,1},{1,0},{2,9},{3,8},{4,17},{5,16},{6,25},{7,24},{8,3},{9,2},{1... | collective-permute-start | bytes 196616 | tf_op jit(solution)/shard_map/ppermute | solution.py:233
  99.9 8.2 %collective-permute-start = (bf16[128,256]{1,0:T(8,128)(2,1)S(1)}, bf16[128,256]{1,0:T(8,128)(2,1)S(1)}, u32[]{:S(2)}, u32[]{:S(2)}) collective-permute-start(bf16[128,256]{1,0:T(8,128)(2,1)S(1)} %get-tuple-element.24), channel_id=1, source_target_pairs={{0,0},{1,1},{2,8},{3,9},{4,16},{5,17},{6,24},{7,25},{8,2},{9,3},{1... | collective-permute-start | bytes 196616 | tf_op jit(solution)/shard_map/ppermute | solution.py:233
  108.9 1.0 copy-start.5
Sparse Core Ops, SparseCore 0:
  72.7 21.8 reduce-scatter.1
